TPU v7x, 32 devices: a whole 2x2x4 slice. The times are simulated.
32 devices in a mesh: fsdp: 4 (over z), ctx: 8 (over y, x, core).
Axes of the slice: x: 2, y: 2, z: 4, core: 2. Of those that a mesh axis runs over, the one named last changes fastest.
Arguments:
- hidden: bfloat16 [4, 1024, 8192], P('fsdp', 'ctx'), may hold values from -6 to 6
- values: bfloat16 [4, 1024, 4096], P('fsdp', 'ctx'), may hold values from -6 to 6
- targets: bfloat16 [4, 1024, 4096], P('fsdp', 'ctx'), may hold values from -6 to 6
- dt_raw: float32 [4, 32, 1024], P('fsdp', None, 'ctx'), as said below
- proj_weight: bfloat16 [8192, 128], P('fsdp'), may hold values from -0.0234375 to 0.0234375
- a_log: float32 [32], replicated
- skip: float32 [32], replicated, may hold values from 0.5 to 1.5
Outputs:
- grad_w: float32 [8192, 128], P('fsdp')
- grad_a_log: float32 [32], replicated
- grad_skip: float32 [32], replicated
- loss: float32 [], replicated
Inputs may be any that keep to these rules, and one draw needn't show every extreme that they name: softplus(dt_raw) is the step size of a head at a position.
All inputs are finite; a program needn't handle non-finite values.
Results may differ from a plain program's by a relative error of at most 0.004.
Values may be sent and summed in bfloat16 or wider, within the bound.
No kernel may reach another device: no remote copies, remote signals or barrier semaphores. Data moves between devices by JAX's collectives and lax.ppermute only.
A program may use at most 192 MiB of HBM per device.

v0:
```python
import math

import jax
import jax.numpy as jnp
from jax import lax
from jax.sharding import PartitionSpec as P

highest = lax.Precision.HIGHEST


def prefix(value, axis, join, neutral, backward):
    count, mine = (lax.axis_size(axis), lax.axis_index(axis))
    pieces = jax.tree.map(lambda part: lax.all_gather(part, axis), value)
    if backward:
        pieces = jax.tree.map(lambda part: part[::-1], pieces)
        mine = count - 1 - mine
    subtotal = jax.tree.map(
        lambda part, zero: jnp.full_like(part, 0) + jnp.asarray(zero, part.dtype), value, neutral
    )

    def hop(position, subtotal):
        longer = join(subtotal, jax.tree.map(lambda part: part[position], pieces))
        return jax.tree.map(lambda new, old: jnp.where(position < mine, new, old), longer, subtotal)

    return lax.fori_loop(0, count - 1, hop, subtotal)


def product(form, left, right):
    return jnp.einsum(form, left, right, preferred_element_type=jnp.float32)


def block_local(proj, step_size, decay_rate, vals, lower_mask):
    row_count = proj.shape[0]
    head_count = step_size.shape[0]
    state_width = proj.shape[1] // 2
    input_map = proj[:, :state_width]
    output_map = proj[:, state_width:]
    decay_sum = jnp.cumsum(step_size * decay_rate[:, None], axis=1)
    final = decay_sum[:, -1:]
    scores = jnp.dot(output_map, input_map.T, preferred_element_type=jnp.float32)
    within = jnp.where(
        lower_mask[None] > 0,
        jnp.exp(jnp.minimum(decay_sum[:, :, None] - decay_sum[:, None, :], 0.0)),
        0.0,
    )
    mixing = within * scores[None] * step_size[:, None, :]
    inputs = vals.reshape(row_count, head_count, vals.shape[1] // head_count)
    inner_out = product("hts,shp->thp", mixing.astype(jnp.bfloat16), inputs)
    to_end = jnp.exp(final - decay_sum)
    weight_end = to_end * step_size
    coef = (weight_end[:, None, :] * input_map.T.astype(jnp.float32)[None]).astype(jnp.bfloat16)
    local_state = product("hns,shp->hnp", coef, inputs)
    growth = jnp.exp(decay_sum)
    carry = jnp.exp(final[:, 0])
    return (
        input_map,
        output_map,
        step_size,
        decay_sum,
        within,
        mixing,
        inputs,
        to_end,
        weight_end,
        growth,
        local_state,
        carry,
        inner_out,
    )


def block_output(pack, state_in, wanted, skip_gain):
    (
        input_map,
        output_map,
        step_size,
        decay_sum,
        within,
        mixing,
        inputs,
        to_end,
        weight_end,
        growth,
        local_state,
        carry,
        inner_out,
    ) = pack
    state_bf = state_in.astype(jnp.bfloat16)
    from_state = product("hnp,tn->thp", state_bf, output_map)
    outputs = (
        inner_out
        + growth.T[:, :, None] * from_state
        + skip_gain[None, :, None] * inputs.astype(jnp.float32)
    )
    misfit = outputs - wanted.reshape(inputs.shape).astype(jnp.float32)
    return (misfit, from_state, state_bf)


def block_return(pack, from_state, state_bf, misfit, loss_scale):
    (
        input_map,
        output_map,
        step_size,
        decay_sum,
        within,
        mixing,
        inputs,
        to_end,
        weight_end,
        growth,
        local_state,
        carry,
        inner_out,
    ) = pack
    grad_out = misfit * loss_scale
    skip_part = jnp.sum(grad_out * inputs.astype(jnp.float32), axis=(0, 2))
    grad_bf = grad_out.astype(jnp.bfloat16)
    mix_grad = product("thp,shp->hts", grad_bf, inputs)
    score_grad = jnp.sum(within * mix_grad * step_size[:, None, :], axis=0)
    weighted = mix_grad * mixing
    sum_grad = (
        jnp.sum(weighted, axis=2)
        - jnp.sum(weighted, axis=1)
        + growth * jnp.sum(grad_out * from_state, axis=2).T
    )
    grown_bf = (growth.T[:, :, None] * grad_out).astype(jnp.bfloat16)
    entry_grad = product("thp,tn->hnp", grown_bf, output_map)
    score_bf = score_grad.astype(jnp.bfloat16)
    out_grad = product("thp,hnp->tn", grown_bf, state_bf) + product(
        "ts,sn->tn", score_bf, input_map
    )
    in_grad = product("ts,tn->sn", score_bf, output_map)
    return (entry_grad, (out_grad, in_grad, sum_grad, skip_part))


def block_finish(pack, partial_value, exit_grad, state_in, decay_rate):
    (
        input_map,
        output_map,
        step_size,
        decay_sum,
        within,
        mixing,
        inputs,
        to_end,
        weight_end,
        growth,
        local_state,
        carry,
        inner_out,
    ) = pack
    out_grad, in_grad, sum_grad, skip_part = partial_value
    exit_bf = exit_grad.astype(jnp.bfloat16)
    coef_grad = product("hnp,shp->hns", exit_bf, inputs)
    in_grad = in_grad + jnp.einsum("hns,hs->sn", coef_grad, weight_end, precision=highest)
    pulled = jnp.einsum("hns,sn->hs", coef_grad, input_map.astype(jnp.float32), precision=highest)
    end_weight = pulled * weight_end
    final_grad = jnp.sum(end_weight, axis=1) + carry * jnp.sum(exit_grad * state_in, axis=(1, 2))
    row_count = step_size.shape[1]
    last_mark = (jnp.arange(row_count) == row_count - 1).astype(jnp.float32)
    sum_grad = sum_grad - end_weight + final_grad[:, None] * last_mark[None, :]
    step_grad = jnp.cumsum(sum_grad[:, ::-1], axis=1)[:, ::-1]
    alog_part = decay_rate * jnp.sum(step_grad * step_size, axis=1)
    proj_grad = jnp.concatenate([in_grad, out_grad], axis=1).astype(jnp.bfloat16)
    return (proj_grad, alog_part, skip_part)


def chain_link(earlier, later):
    return (earlier[0] * later[0], later[1] + later[0][:, None, None] * earlier[1])


def local(hidden, values, targets, dt_raw, proj_weight, a_log, skip):
    row_count = hidden.shape[1]
    features = hidden[0]
    position = jnp.arange(row_count)
    lower_mask = (position[:, None] >= position[None, :]).astype(jnp.float32)
    picked = features
    projection = jnp.dot(
        picked,
        lax.all_gather(proj_weight, "fsdp", axis=0, tiled=True),
        preferred_element_type=jnp.float32,
    )
    proj_bf = projection.astype(jnp.bfloat16)
    step_size = jax.nn.softplus(dt_raw[0])
    decay_rate = -jnp.exp(a_log)
    sequences = lax.axis_size("fsdp")
    length = row_count * lax.axis_size("ctx")
    loss_scale = 1.0 / (values.shape[2] * math.sqrt(sequences * length))
    local_pack = block_local(proj_bf, step_size, decay_rate, values[0], lower_mask)
    carry = local_pack[11]
    local_state = local_pack[10]
    identity = (jnp.ones_like(carry), jnp.zeros_like(local_state))
    entry = prefix((carry, local_state), "ctx", chain_link, identity, False)
    state_in = entry[1]
    misfit, from_state, state_bf = block_output(local_pack, state_in, targets[0], skip)
    loss_part = 0.5 * loss_scale * jnp.sum(misfit * misfit)
    entry_grad, partial_value = block_return(local_pack, from_state, state_bf, misfit, loss_scale)
    later = prefix((carry, entry_grad), "ctx", chain_link, identity, True)
    proj_grad, alog_part, skip_part = block_finish(
        local_pack, partial_value, later[1], state_in, decay_rate
    )
    picked = features
    shard_grad = lax.psum_scatter(
        lax.dot_general(
            picked, proj_grad, (((0,), (0,)), ((), ())), preferred_element_type=jnp.float32
        ),
        "fsdp",
        scatter_dimension=0,
        tiled=True,
    )
    grad_w = lax.psum(shard_grad, "ctx")
    totals = lax.psum((loss_part, alog_part, skip_part), ("fsdp", "ctx"))
    return (grad_w, totals[1], totals[2], totals[0])


def solution(mesh):
    in_specs = (
        P("fsdp", "ctx", None),
        P("fsdp", "ctx", None),
        P("fsdp", "ctx", None),
        P("fsdp", None, "ctx"),
        P("fsdp", None),
        P(),
        P(),
    )
    out_specs = (P("fsdp", None), P(), P(), P())
    return jax.shard_map(local, mesh=mesh, in_specs=in_specs, out_specs=out_specs, check_vma=False)
```

profile of v0, /device:TPU:0, one launch (start us, length us, event | category | flops | bytes accessed | tf_op | source)
XLA Modules:
  0.0 367.6 jit_solution(10082568660013058788)
XLA Ops:
  7.2 0.7 all-gather.7.cloned.1.call-update
  8.0 1.6 copy.31
  9.7 0.3 reduce_window_sum.17
  10.0 0.2 fusion.50
  10.3 48.0 %all-gather.7.cloned.1.call-done = bf16[8192,128]{1,0:T(8,128)(2,1)} async-done(((bf16[2048,128]{1,0:T(8,128)(2,1)}), bf16[8192,128]{1,0:T(8,128)(2,1)}) %all-gather.7.cloned.1.call-update) | async-done | bytes 2097168 | tf_op jit(solution)/shard_map/all_gather | solution.py:180
  58.3 2.5 fusion.12
  60.8 1.8 fusion.27
  62.7 0.6 dynamic-slice
  64.0 0.2 dynamic-update-slice
  64.2 13.8 %all-reduce = f32[256]{0:T(256)S(1)} all-reduce(f32[256]{0:T(256)S(1)} %dynamic-update-slice), channel_id=3, replica_groups=mesh['fsdp'=4,'ctx'=8] {'ctx'}, use_global_device_ids=true, to_apply=%add | all-reduce | flops 256 | bytes 2048
  78.1 2.6 copy.33
  81.0 35.0 %all-gather.9.cloned.1.call-done = f32[256,64,128]{2,1,0:T(8,128)} async-done(((f32[32,64,128]{2,1,0:T(8,128)}), f32[256,64,128]{2,1,0:T(8,128)}) %all-gather.9.cloned.1.call-update) | async-done | bytes 8388624 | tf_op jit(solution)/shard_map/all_gather | solution.py:13
  116.0 10.5 %while.28 = (s32[]{:T(128)}, f32[32,64,128]{2,1,0:T(8,128)S(1)}, s32[]{:T(128)}, f32[8,32,64,128]{3,2,1,0:T(8,128)}, f32[8,32]{1,0:T(8,128)S(1)}, /*index=5*/s32[]{:T(128)}, s32[]{:T(128)}) while((s32[]{:T(128)}, f32[32,64,128]{2,1,0:T(8,128)S(1)}, s32[]{:T(128)}, f32[8,32,64,128]{3,2,1,0:T(8,128)}, f32[8,32]{1,0:T(8,128)S(1)}, ...), condition=%wide.region_2.3_spmd.clone, body=%wide.region_1.2_spmd.clone.sunk | while | flops 1048580 | bytes 3146225 | solution.py:25
  116.0 1.5 fusion.73
  117.5 1.5 fusion.73
  119.0 1.5 fusion.73
  120.5 1.5 fusion.73
  122.0 1.5 fusion.73
  123.6 1.5 fusion.73
  125.1 1.5 fusion.73
  126.6 0.5 fusion.33
  127.1 0.6 copy-done.2
  127.8 0.7 copy-done.5
  128.5 2.4 multiply_reduce_fusion
  130.8 1.3 copy-done.3
  132.2 1.5 convolution_bitcast_fusion.1
  133.7 3.7 fusion.10
  137.6 0.4 fusion.17
  137.9 50.3 %all-gather.11.cloned.1.call-done = f32[256,64,128]{2,1,0:T(8,128)} async-done(((f32[32,64,128]{2,1,0:T(8,128)}), f32[256,64,128]{2,1,0:T(8,128)}) %all-gather.11.cloned.1.call-update) | async-done | bytes 8388624 | tf_op jit(solution)/shard_map/all_gather | solution.py:13
  188.2 8.3 %rev.12 = f32[8,32,64,128]{3,2,1,0:T(8,128)} reverse(f32[8,32,64,128]{3,2,1,0:T(8,128)} %bitcast.112), dimensions={0} | reverse | bytes 16777216 | tf_op jit(solution)/shard_map/rev | solution.py:15
  196.5 18.8 %while.29 = (s32[]{:T(128)}, f32[32,64,128]{2,1,0:T(8,128)}, s32[]{:T(128)}, f32[8,32,64,128]{3,2,1,0:T(8,128)}, f32[8,32]{1,0:T(8,128)S(1)}, /*index=5*/s32[]{:T(128)}, s32[]{:T(128)}) while((s32[]{:T(128)}, f32[32,64,128]{2,1,0:T(8,128)}, s32[]{:T(128)}, f32[8,32,64,128]{3,2,1,0:T(8,128)}, f32[8,32]{1,0:T(8,128)S(1)}, ...), condition=%wide.region_5.6_spmd.clone, body=%wide.region_4.5_spmd.clone.sunk | while | flops 1048580 | bytes 3146225 | solution.py:25
  196.5 2.4 fusion.74
  198.9 2.7 fusion.74
  201.6 2.7 fusion.74
  204.4 2.7 fusion.74
  207.1 2.7 fusion.74
  209.8 2.7 fusion.74
  212.6 2.7 fusion.74
  215.3 3.0 multiply_reduce_fusion.4
  218.4 2.6 convolution_bitcast_fusion
  221.8 1.3 multiply_reduce_fusion.3
  223.3 1.6 multiply_reduce_fusion.5
  224.9 0.2 add_reduce_fusion
  225.1 72.8 %reduce-scatter.2.cloned.1.call-done = f32[2048,128]{0,1:T(8,128)} async-done(((f32[8192,128]{0,1:T(8,128)}), f32[2048,128]{0,1:T(8,128)}) %reduce-scatter.2.cloned.1.call-update) | async-done | bytes 1048592 | tf_op jit(solution)/shard_map/reduce_scatter | solution.py:203
  298.1 0.3 reduce_window_sum.18
  298.7 40.8 %all-reduce.1 = (f32[32]{0:T(128)}, f32[32]{0:T(128)}, f32[]{:T(128)}) all-reduce(f32[32]{0:T(128)S(1)} %fusion.63, f32[32]{0:T(128)S(1)} %get-tuple-element.247, f32[]{:T(128)S(6)} %mul_shard_map.3), channel_id=1, replica_groups=mesh['fsdp'=4,'ctx'=8] {'fsdp','ctx'}, use_global_device_ids=true, to_apply=%region_15.16 | all-reduce | flops 65 | bytes 520 | tf_op jit(solution)/shard_map/psum | solution.py:212
  339.5 19.0 %all-reduce.4.cloned.1.call-done = f32[2048,128]{0,1:T(8,128)} async-done(((f32[2048,128]{0,1:T(8,128)}), f32[2048,128]{0,1:T(8,128)}) %all-reduce.4.cloned.1.call-update) | async-done | bytes 1048592 | tf_op jit(solution)/shard_map/psum | solution.py:211
  358.5 2.5 copy.41
  (63 shorter events, 1.8 us)
Async XLA Ops:
  7.2 51.1 %copy-start = (bf16[1,128,8192]{2,1,0:T(8,128)(2,1)S(1)}, bf16[1,128,8192]{2,1,0:T(8,128)(2,1)}, u32[]{:S(2)}) copy-start(bf16[1,128,8192]{2,1,0:T(8,128)(2,1)} %param.11) | copy-start | bytes 6291460
  7.2 2.4 copy-start.8
  7.2 2.5 copy-start.6
  7.2 51.1 %all-gather.7.cloned.1.call-start = ((), (), s32[]{:S(2)}) async-start(), calls=%async_computation.1 | async-start | bytes 2621440 | tf_op jit(solution)/shard_map/all_gather | solution.py:180
  7.9 108.1 %all-gather.9.cloned.1.call-start = ((), (), s32[]{:S(2)}) async-start(), calls=%async_computation.4 | async-start | bytes 9437184 | tf_op jit(solution)/shard_map/all_gather | solution.py:13
  9.6 51.2 %copy-start.1 = (bf16[1,128,4096]{1,2,0:T(8,128)(2,1)}, bf16[1,128,4096]{1,2,0:T(8,128)(2,1)S(1)}, u32[]{:S(2)}) copy-start(bf16[1,128,4096]{1,2,0:T(8,128)(2,1)S(1)} %copy.31) | copy-start | bytes 3145732
  60.8 1.9 copy-start.9
  62.7 125.5 %all-gather.11.cloned.1.call-start = ((), (), s32[]{:S(2)}) async-start(), calls=%async_computation.5 | async-start | bytes 9437184 | tf_op jit(solution)/shard_map/all_gather | solution.py:13
  126.5 1.2 copy-start.2
  126.5 1.9 copy-start.5
  126.6 1.9 copy-start.7
  130.8 1.4 copy-start.3
  133.7 164.3 %reduce-scatter.2.cloned.1.call-start = ((), (), s32[]{:S(2)}) async-start(), calls=%async_computation.2 | async-start | bytes 5242880 | tf_op jit(solution)/shard_map/reduce_scatter | solution.py:203
  133.7 3.8 %copy-start.4 = (f32[128,32,128]{0,2,1:T(8,128)S(1)}, f32[128,32,128]{0,2,1:T(8,128)}, u32[]{:S(2)}) copy-start(f32[128,32,128]{0,2,1:T(8,128)} %copy-done.3) | copy-start | bytes 6291460
  221.0 137.5 %all-reduce.4.cloned.1.call-start = ((), (), s32[]{:S(2)}) async-start(), calls=%async_computation.3 | async-start | bytes 2097152 | tf_op jit(solution)/shard_map/psum | solution.py:211
Sparse Core Ops, SparseCore 0:
  9.6 48.6 all-gather.6
  62.8 53.1 all-gather.8
  133.8 54.3 all-gather.10
  221.2 76.7 reduce-scatter.1
  301.3 57.1 all-reduce.3
where the time goes:
time: 369 us; the launch traced here: 368 us
  waiting for transfers between devices  226 us (61%)
  blocking collectives  54.6 us (15%)
  other arithmetic  33.2 us (9%)
  local copies, waits for them, and re-layouts  19.3 us (5%)
  matrix products  18.8 us (5%)
  between operations  15.3 us (4%)
    all_gather x2, waiting for transfers between devices, prefix(): pieces = jax.tree.map(lambda part: lax.all_gather(part, axis), value)  85.3 us
    reduce_scatter x1, waiting for transfers between devices, local(): lax.psum_scatter(lax.dot_general(picked, proj_grad, (((0,), (0,)), ((), (...  72.8 us
    all_gather x1, waiting for transfers between devices, local(): lax.all_gather(proj_weight, 'fsdp', axis=0, tiled=True)  48 us
    psum x1, blocking collectives, local(): totals = lax.psum((loss_part, alog_part, skip_part), ('fsdp', 'ctx'))  40.8 us
    select_n x14, other arithmetic, hop(): jnp.where(position < mine, new, old)  29 us
    psum x1, waiting for transfers between devices, local(): grad_w = lax.psum(shard_grad, 'ctx')  19 us
    unnamed x1, blocking collectives  13.8 us
    dot_general x9, matrix products, product(): return jnp.einsum(form, left, right, preferred_element_type=jnp.float32)  13.4 us
  transfers between devices with their start and end apart: 5, of which 5 were waited for; matrix products, arithmetic and copies ran while one was open for 4% of the time, Pallas kernels for 0%

commit v1 on v0

v1 whole, which is shorter than its diff:
```python
import functools
import math

import jax
import jax.numpy as jnp
from jax import lax
from jax.experimental import pallas as pl
from jax.experimental.pallas import tpu as pltpu
from jax.sharding import PartitionSpec as P

BLOCK = 128
HDIM = 128
PAD = 16


def dot(left, right, dims):
    return lax.dot_general(left, right, (dims, ((), ())), preferred_element_type=jnp.float32)


def fold(value):
    return jnp.sum(value.reshape(value.shape[0] // 8, 8, value.shape[1]), axis=0)


def pieces(value):
    high = value.astype(jnp.bfloat16)
    rest = value - high.astype(jnp.float32)
    middle = rest.astype(jnp.bfloat16)
    return high, middle, (rest - middle.astype(jnp.float32)).astype(jnp.bfloat16)


def running_sum(value):
    lane = lax.broadcasted_iota(jnp.int32, value.shape, 1)
    shift = 1
    while shift < value.shape[1]:
        value += jnp.where(lane >= shift, pltpu.roll(value, shift, 1), 0.0)
        shift *= 2
    return value


def softplus(value):
    small = jnp.exp(-jnp.abs(value))
    series = small * (1.0 - small * (0.5 - small * (1 / 3 - small * (0.25 - small * 0.2))))
    return jnp.maximum(value, 0.0) + jnp.where(small < 0.03, series, jnp.log1p(small))


def prepare_kernel(
    heads, vt_ref, rate_ref, skip_ref, v_ref, within_ref, sloped_ref, base_ref, weighed_ref,
    cols_ref, carry_ref, last_ref, rows_ref,
):
    blocks, tail_at, width = vt_ref.shape[0], vt_ref.shape[1] - PAD, vt_ref.shape[2]
    t_at = lax.broadcasted_iota(jnp.int32, (BLOCK, BLOCK), 0)
    s_at = lax.broadcasted_iota(jnp.int32, (BLOCK, BLOCK), 1)
    mask = t_at >= s_at
    sent = []
    for k in range(blocks):
        rows = vt_ref[k, tail_at:, :].astype(jnp.float32)
        sent.append(rows[:heads] + rows[heads : 2 * heads] + rows[2 * heads : 3 * heads])
    step = softplus(jnp.concatenate(sent, axis=0))
    decay = running_sum(step * rate_ref[...])
    decay_c, step_c = decay.T, step.T
    tail_c = decay_c[BLOCK - 1 :, :] - decay_c
    growth_c = jnp.exp(decay_c)
    end_c = jnp.exp(tail_c) * step_c
    rise_c = growth_c * decay_c

    def spread(row):
        each = [jnp.broadcast_to(row[:, h : h + 1], (1, width)) for h in range(heads)]
        return jnp.concatenate(each, axis=1)

    for k in range(blocks):
        own = slice(k * heads, (k + 1) * heads)
        made = (growth_c, rise_c, end_c, tail_c, decay_c)
        cols_ref[k] = jnp.concatenate([x[:, own] for x in made], axis=1)
        rows_ref[k, :heads, :] = decay[own, :]
        rows_ref[k, heads:, :] = step[own, :]
        carry_ref[k] = spread(growth_c[BLOCK - 1 :, own])
        last_ref[k] = spread(rise_c[BLOCK - 1 :, own])

    def block(k, carry):
        cols, rows = cols_ref[k], rows_ref[k]
        for h in range(heads):
            i = k * heads + h
            col = lambda j: cols[:, j * heads + h : j * heads + h + 1]
            diff = jnp.minimum(col(4) - rows[h : h + 1, :], 0.0)
            within = jnp.where(mask, jnp.exp(diff), 0.0) * rows[heads + h : heads + h + 1, :]
            within_ref[i] = within
            sloped_ref[i] = within * diff
            v = vt_ref[k, h * BLOCK : (h + 1) * BLOCK, :]
            goal = vt_ref[k, (heads + h) * BLOCK : (heads + h + 1) * BLOCK, :]
            vf = v.astype(jnp.float32)
            v_ref[i] = v
            base_ref[i] = skip_ref[h] * vf - goal.astype(jnp.float32)
            weighed_ref[k, :, h * width : (h + 1) * width] = (vf * col(2)).astype(jnp.bfloat16)
        return carry

    lax.fori_loop(0, blocks, block, 0)


def mixer_kernel(
    heads, scale, count, maps_ref, v_ref, within_ref, sloped_ref, base_ref, weighed_ref, cols_ref,
    carry_ref, last_ref, first_ref, out_ref, pack_ref, states, entries, parts, stat_ref,
):
    blocks, width = cols_ref.shape[0], v_ref.shape[2]
    half = maps_ref.shape[1] // 2
    full = heads * width
    stat_ref[...] = jnp.zeros_like(stat_ref)

    def forward(k, state):
        at = pl.ds(pl.multiple_of(k * BLOCK, BLOCK), BLOCK)
        maps, cols = maps_ref[at, :], cols_ref[k]
        b, c = maps[:, :half], maps[:, half:]
        scores = dot(c, b, ((1,), (1,)))
        state_bf = state.astype(jnp.bfloat16)
        states[k] = state
        from_all = dot(c, state_bf, ((1,), (0,)))
        score_grad = jnp.zeros((BLOCK, BLOCK), jnp.float32)
        grown = []
        for h in range(heads):
            i = k * heads + h
            v, within = v_ref[i], within_ref[i]
            growth, rise = cols[:, h : h + 1], cols[:, heads + h : heads + h + 1]
            inner = dot((within * scores).astype(jnp.bfloat16), v, ((1,), (0,)))
            from_state = from_all[:, h * width : (h + 1) * width]
            misfit = inner + growth * from_state + base_ref[i]
            grad = misfit * scale
            mix_grad = dot(grad.astype(jnp.bfloat16), v, ((1,), (1,)))
            grown.append((grad * growth).astype(jnp.bfloat16))
            stat_ref[h, 0] += fold(misfit * misfit)
            stat_ref[h, 1] += fold(grad * v.astype(jnp.float32))
            stat_ref[h, 2] += fold(grad * from_state * rise)
            score_grad += within * mix_grad
            stat_ref[h, 2] += fold(mix_grad * scores * sloped_ref[i])
        grown = jnp.concatenate(grown, axis=1)
        entries[k] = dot(c, grown, ((0,), (0,)))
        score_bf = score_grad.astype(jnp.bfloat16)
        grad_c = dot(grown, state_bf, ((1,), (1,))) + dot(score_bf, b, ((1,), (0,)))
        grad_b = dot(score_bf, c, ((0,), (0,)))
        parts[at, :] = jnp.concatenate([grad_b, grad_c], axis=1)
        return carry_ref[k] * state + dot(b, weighed_ref[k], ((0,), (0,)))

    unrolled(blocks, forward, jnp.zeros((half, full), jnp.float32))

    def backward(i, leaving):
        k = blocks - 1 - i
        at = pl.ds(pl.multiple_of(k * BLOCK, BLOCK), BLOCK)
        bf = maps_ref[at, :][:, :half].astype(jnp.float32)
        cols = cols_ref[k]
        leaving_bf = leaving.astype(jnp.bfloat16)
        grad_b = jnp.zeros((BLOCK, half), jnp.float32)
        overlap = leaving * states[k] * last_ref[k]
        for h in range(heads):
            piece = slice(h * width, (h + 1) * width)
            coef_grad = dot(v_ref[k * heads + h], leaving_bf[:, piece], ((1,), (1,)))
            pulled = coef_grad * cols[:, 2 * heads + h : 2 * heads + h + 1]
            grad_b += pulled
            tail = cols[:, 3 * heads + h : 3 * heads + h + 1]
            stat_ref[h, 2, :, :half] += fold(pulled * bf * tail)
            stat_ref[h, 2] += fold(overlap[:, piece])
        both = jnp.concatenate([grad_b, jnp.zeros_like(grad_b)], axis=1)
        out_ref[at, :] = (parts[at, :] + both).astype(out_ref.dtype)
        return entries[k] + carry_ref[k] * leaving

    unrolled(blocks, backward, jnp.zeros((half, full), jnp.float32))

    lane = lax.broadcasted_iota(jnp.int32, (1, 128), 1)
    packed = jnp.zeros((1, 128), jnp.float32)
    for h in range(heads):
        at_head = first_ref[0] + h
        sums = [jnp.sum(stat_ref[h, i]) for i in range(3)]
        packed += jnp.where(lane == at_head, sums[2], 0.0)
        packed += jnp.where(lane == count + at_head, sums[1], 0.0)
        packed += jnp.where(lane == 2 * count, 0.5 * scale * sums[0], 0.0)
    pack_ref[...] = jnp.zeros_like(pack_ref)
    for i, piece in enumerate(pieces(packed)):
        pack_ref[i : i + 1, :] = piece


def unrolled(count, step, start):
    each = 4 if count % 4 == 0 else 1

    def several(i, value):
        for j in range(each):
            value = step(i * each + j, value)
        return value

    return lax.fori_loop(0, count // each, several, start)


VMEM = pl.BlockSpec(memory_space=pltpu.VMEM)
SMEM = pl.BlockSpec(memory_space=pltpu.SMEM)
ANY = pl.BlockSpec(memory_space=pl.ANY)
LIMIT = 28 * 1024 * 1024


def prepare(vt, rates, skip):
    blocks, rows, width = vt.shape
    heads = (rows - PAD) // BLOCK // 2
    units, full = blocks * heads, heads * width
    square = jax.ShapeDtypeStruct((units, BLOCK, BLOCK), jnp.float32)
    row = jax.ShapeDtypeStruct((blocks, 1, full), jnp.float32)
    return pl.pallas_call(
        functools.partial(prepare_kernel, heads),
        out_shape=(
            jax.ShapeDtypeStruct((units, BLOCK, width), jnp.bfloat16),
            square,
            square,
            jax.ShapeDtypeStruct((units, BLOCK, width), jnp.float32),
            jax.ShapeDtypeStruct((blocks, BLOCK, full), jnp.bfloat16),
            jax.ShapeDtypeStruct((blocks, BLOCK, 5 * heads), jnp.float32),
            row,
            row,
        ),
        in_specs=[VMEM, VMEM, SMEM],
        out_specs=(VMEM,) * 8,
        scratch_shapes=[pltpu.VMEM((blocks, 2 * heads, BLOCK), jnp.float32)],
        compiler_params=pltpu.CompilerParams(vmem_limit_bytes=LIMIT),
        name="prepare",
    )(vt, rates, skip)


def mixer(maps, ready, first, scale, count):
    length, both = maps.shape
    units, _, width = ready[0].shape
    blocks = length // BLOCK
    heads = units // blocks
    full = heads * width
    return pl.pallas_call(
        functools.partial(mixer_kernel, heads, scale, count),
        out_shape=(
            jax.ShapeDtypeStruct((length, both), jnp.bfloat16),
            jax.ShapeDtypeStruct((PAD, 128), jnp.bfloat16),
        ),
        in_specs=[VMEM] * 9 + [SMEM],
        out_specs=(VMEM, VMEM),
        scratch_shapes=[
            pltpu.VMEM((blocks, both // 2, full), jnp.float32),
            pltpu.VMEM((blocks, both // 2, full), jnp.float32),
            pltpu.VMEM((length, both), jnp.float32),
            pltpu.VMEM((heads, 3, 8, 128), jnp.float32),
        ],
        compiler_params=pltpu.CompilerParams(vmem_limit_bytes=LIMIT),
        cost_estimate=pl.CostEstimate(
            flops=14 * length * BLOCK * full, bytes_accessed=6 * length * full, transcendentals=0
        ),
        name="mixer",
    )(maps, *ready, first.reshape(1))


def pack_mixer_kernel(
    core_ref, values_hbm, targets_hbm, dt_ref, weight_hbm, out_hbm, part_ref, held, out_ref,
    weight_sem, in_sems, sems,
):
    count, rows, width = out_ref.shape
    heads = (rows - PAD) // BLOCK // 2
    loads = []
    for c in range(count):
        own = pl.ds(c * heads * width, heads * width)
        for i, ref in enumerate((values_hbm, targets_hbm)):
            copy = pltpu.make_async_copy(ref.at[0, :, own], held.at[c, i], in_sems.at[c, i])
            copy.start()
            loads.append(copy)
    half = part_ref.shape[0]
    at = pl.multiple_of(core_ref[0] * half, half)
    load = pltpu.make_async_copy(weight_hbm.at[pl.ds(at, half), :], part_ref, weight_sem)
    load.start()
    for c in range(count):
        sent = [x.astype(jnp.float32) for x in pieces(dt_ref[0, c * heads : (c + 1) * heads, :])]
        sent.append(jnp.zeros((PAD - 3 * heads, width), jnp.float32))
        out_ref[c, rows - PAD :, :] = jnp.concatenate(sent, axis=0).astype(jnp.bfloat16)
    stores = []
    for c in range(count):
        for i in range(2):
            loads[2 * c + i].wait()
            for h in range(heads):
                to = (i * heads + h) * BLOCK
                out_ref[c, to : to + BLOCK, :] = held[c, i, :, h * width : (h + 1) * width]
        stores.append(pltpu.make_async_copy(out_ref.at[c], out_hbm.at[c], sems.at[c]))
        stores[c].start()
    load.wait()
    for copy in stores:
        copy.wait()


def pack_mixer(core, values, targets, dt_raw, weight, ctx):
    rows, width = values.shape[1:]
    heads = dt_raw.shape[1] // ctx
    shape = (ctx, 2 * heads * BLOCK + PAD, HDIM)
    return pl.pallas_call(
        pack_mixer_kernel,
        out_shape=(
            jax.ShapeDtypeStruct(shape, jnp.bfloat16),
            jax.ShapeDtypeStruct((weight.shape[0] // 2, weight.shape[1]), jnp.bfloat16),
        ),
        in_specs=[SMEM, ANY, ANY, VMEM, ANY],
        out_specs=(ANY, VMEM),
        scratch_shapes=[
            pltpu.VMEM((ctx, 2, rows, width // ctx), jnp.bfloat16),
            pltpu.VMEM(shape, jnp.bfloat16),
            pltpu.SemaphoreType.DMA,
            pltpu.SemaphoreType.DMA((ctx, 2)),
            pltpu.SemaphoreType.DMA((ctx,)),
        ],
        name="pack_mixer",
    )(core.reshape(1), values, targets, dt_raw, weight)


def pack_hidden_kernel(half, core_ref, hidden_ref, out_ref):
    for f in range(out_ref.shape[1] // half):
        at = pl.multiple_of((2 * f + core_ref[0]) * half, half)
        out_ref[:, f * half : (f + 1) * half] = hidden_ref[0, :, pl.ds(at, half)]


def pack_hidden(core, hidden, half):
    _, rows, width = hidden.shape
    return pl.pallas_call(
        functools.partial(pack_hidden_kernel, half),
        out_shape=jax.ShapeDtypeStruct((rows, width // 2), jnp.bfloat16),
        in_specs=[SMEM, VMEM],
        out_specs=VMEM,
        compiler_params=pltpu.CompilerParams(vmem_limit_bytes=LIMIT),
        name="pack_hidden",
    )(core.reshape(1), hidden)


def project_kernel(half, chunk_ref, hidden_ref, start_ref, *refs):
    weights, out_ref = refs[:-1], refs[-1]
    total = start_ref[...]
    j = 0
    for weight_ref in weights:
        for i in range(weight_ref.shape[0] // half):
            at = pl.multiple_of(chunk_ref[j] * half, half)
            block = weight_ref[i * half : (i + 1) * half, :]
            total += dot(hidden_ref[0, :, pl.ds(at, half)], block, ((1,), (0,)))
            j += 1
    out_ref[...] = total.astype(out_ref.dtype)


def project(chunks, hidden, weights, start, kind):
    half = sum(weight.shape[0] for weight in weights) // len(chunks)
    return pl.pallas_call(
        functools.partial(project_kernel, half),
        out_shape=jax.ShapeDtypeStruct(start.shape, kind),
        in_specs=[SMEM] + [VMEM] * (2 + len(weights)),
        out_specs=VMEM,
        compiler_params=pltpu.CompilerParams(vmem_limit_bytes=LIMIT),
        name="project",
    )(jnp.stack(chunks).astype(jnp.int32), hidden, start, *weights)


def put_scalars(out_ref, at, tails):
    parts = pieces(jnp.sum(tails, axis=0, keepdims=True))
    out_ref[at:, :] = jnp.zeros((PAD, out_ref.shape[1]), out_ref.dtype)
    for i, part in enumerate(parts):
        out_ref[at + i : at + i + 1, :] = part


def grad_kernel(half, core_ref, near_ref, far_ref, hidden_ref, feats_ref, out_ref):
    chips = out_ref.shape[0]
    slab = half // chips
    step = max(slab, 128)
    near, far = [
        [ref[i * BLOCK : (i + 1) * BLOCK, :] for i in range(2)] for ref in (near_ref, far_ref)
    ]
    for f in range(feats_ref.shape[1] // half):
        for at in range(0, half, step):
            mine = pl.multiple_of((2 * f + core_ref[0]) * half + at, step)
            near_feats = hidden_ref[0, :, pl.ds(mine, step)]
            far_feats = feats_ref[:, f * half + at : f * half + at + step]
            turned = sum(dot(part, near_feats, ((0,), (0,))) for part in near)
            turned += sum(dot(part, far_feats, ((0,), (0,))) for part in far)
            turned = turned.T.astype(out_ref.dtype)
            for i in range(step // slab):
                rows = turned[i * slab : (i + 1) * slab]
                out_ref[at // slab + i, f * slab : (f + 1) * slab, :] = rows
    tails = [ref[2 * BLOCK :, :].astype(jnp.float32) for ref in (near_ref, far_ref)]
    for q in range(chips):
        put_scalars(out_ref.at[q], out_ref.shape[1] - PAD, tails[0] + tails[1])


def weight_grad(core, near, far, hidden, feats, half, chips):
    fsdp = feats.shape[1] // half
    rows = fsdp * half // chips + PAD
    return pl.pallas_call(
        functools.partial(grad_kernel, half),
        out_shape=jax.ShapeDtypeStruct((chips, rows, near.shape[1]), jnp.bfloat16),
        in_specs=[SMEM] + [VMEM] * 4,
        out_specs=VMEM,
        compiler_params=pltpu.CompilerParams(vmem_limit_bytes=LIMIT),
        name="weight_grad",
    )(core.reshape(1), near, far, hidden, feats)


def add_chips_kernel(grad_ref, out_ref):
    fsdp, slab = out_ref.shape[0], out_ref.shape[1] - PAD
    total = jnp.sum(grad_ref[...].astype(jnp.float32), axis=0)
    for f in range(fsdp):
        out_ref[f, :slab, :] = total[f * slab : (f + 1) * slab].astype(out_ref.dtype)
        put_scalars(out_ref.at[f], slab, total[fsdp * slab :])


def add_chips(grad, fsdp):
    _, rows, width = grad.shape
    return pl.pallas_call(
        add_chips_kernel,
        out_shape=jax.ShapeDtypeStruct((fsdp, (rows - PAD) // fsdp + PAD, width), jnp.bfloat16),
        in_specs=[VMEM],
        out_specs=VMEM,
        compiler_params=pltpu.CompilerParams(vmem_limit_bytes=LIMIT),
        name="add_chips",
    )(grad)


def add_kernel(grad_ref, out_ref, alog_ref, skip_ref, loss_ref):
    count, slab = grad_ref.shape[0], out_ref.shape[0]
    heads = alog_ref.shape[1]
    total = jnp.sum(grad_ref[...].astype(jnp.float32), axis=0)
    out_ref[...] = total[:slab].astype(out_ref.dtype)
    total = jnp.sum(total[slab:], axis=0, keepdims=True)
    alog_ref[...] = total[:, :heads]
    skip_ref[...] = total[:, heads : 2 * heads]
    loss_ref[...] = total[:, 2 * heads : 2 * heads + 1]


def add_blocks(grad, heads):
    _, rows, width = grad.shape
    return pl.pallas_call(
        add_kernel,
        out_shape=(
            jax.ShapeDtypeStruct((rows - PAD, width), jnp.bfloat16),
            jax.ShapeDtypeStruct((1, heads), jnp.float32),
            jax.ShapeDtypeStruct((1, heads), jnp.float32),
            jax.ShapeDtypeStruct((1, 1), jnp.float32),
        ),
        in_specs=[VMEM],
        out_specs=(VMEM,) * 4,
        compiler_params=pltpu.CompilerParams(vmem_limit_bytes=LIMIT),
        name="add_blocks",
    )(grad)


def finish_kernel(grad_ref, out_ref):
    count = grad_ref.shape[0]
    for q in range(count // 2):
        for r in range(2):
            out_ref[r * (count // 2) + q] = grad_ref[2 * q + r].astype(jnp.float32)


def finish(grad):
    return pl.pallas_call(
        finish_kernel,
        out_shape=jax.ShapeDtypeStruct(grad.shape, jnp.float32),
        in_specs=[VMEM],
        out_specs=VMEM,
        compiler_params=pltpu.CompilerParams(vmem_limit_bytes=LIMIT),
        name="finish",
    )(grad)


def exchange(blocks, axis):
    return lax.all_to_all(blocks, axis, 0, 0, tiled=True)


def swap(block, axis, shift):
    return lax.ppermute(block, axis, [(i, i ^ shift) for i in range(lax.axis_size(axis))])


def local(hidden, values, targets, dt_raw, proj_weight, a_log, skip):
    fsdp, ctx = lax.axis_size("fsdp"), lax.axis_size("ctx")
    mine = lax.axis_index("ctx")
    core = mine % 2
    rows = hidden.shape[1]
    length = rows * ctx
    heads_all = a_log.shape[0]
    inner = values.shape[2]
    cols = inner // ctx
    heads = cols // HDIM
    half = proj_weight.shape[0] // 2
    slab = proj_weight.shape[0] // ctx
    both = proj_weight.shape[1]
    first = mine * heads
    scale = 1.0 / (inner * math.sqrt(fsdp * length))

    shard = lax.axis_index("fsdp")
    others = [shard ^ shift for shift in range(1, fsdp)]

    vt, part = pack_mixer(core, values, targets, dt_raw, proj_weight, ctx)
    near = [swap(part, "fsdp", shift) for shift in range(1, fsdp)]
    vt = exchange(vt, "ctx")
    a_mine = lax.dynamic_slice_in_dim(a_log, first, heads, 0)
    s_mine = lax.dynamic_slice_in_dim(skip, first, heads, 0)
    rates = jnp.tile(-jnp.exp(a_mine), ctx)[:, None]
    send = pack_hidden(1 - core, hidden, half)
    start = jnp.zeros((rows, both), jnp.float32)
    start = project([2 * shard, 2 * shard + 1], hidden, [proj_weight], start, jnp.float32)
    near, send, rates, s_mine, start = lax.optimization_barrier(
        (near, send, rates, s_mine, start)
    )
    far = [swap(block, "ctx", 1) for block in near]

    near_at = [2 * other + core for other in others]
    far_at = [2 * other + 1 - core for other in others]
    chunks = [at[i] for i in range(fsdp - 1) for at in (near_at, far_at)]
    blocks = [part[i] for i in range(fsdp - 1) for part in (near, far)]
    projection = project(chunks, hidden, blocks, start, jnp.bfloat16)
    projection, vt = lax.optimization_barrier((projection, vt))
    maps = lax.all_gather(projection, "ctx", axis=0, tiled=True)
    maps, send = lax.optimization_barrier((maps, send))
    feats = swap(send, "ctx", 1)

    ready = prepare(vt, rates, s_mine)
    proj_part, packed = mixer(maps, ready, first, scale, heads_all)

    proj_part = exchange(proj_part.reshape(ctx, rows, both), "ctx").astype(jnp.float32)
    proj_grad = jnp.sum(proj_part, axis=0)
    high = lax.reduce_precision(proj_grad, 8, 7)
    proj_grad = [part.astype(jnp.bfloat16) for part in (high, proj_grad - high)]
    proj_grad = jnp.concatenate(proj_grad + [packed], axis=0)
    proj_far = swap(proj_grad, "ctx", 1)

    grad = weight_grad(core, proj_grad, proj_far, hidden, feats, half, ctx // 2)
    chips = [list(range(r, ctx, 2)) for r in range(2)]
    grad = lax.all_to_all(grad, "ctx", 0, 0, tiled=True, axis_index_groups=chips)
    grad = exchange(add_chips(grad, fsdp), "fsdp")
    grad, grad_a, grad_skip, loss = add_blocks(grad, heads_all)
    grad_w = finish(lax.all_gather(grad, "ctx", axis=0)).reshape(ctx * slab, both)
    return (grad_w, grad_a.reshape(heads_all), grad_skip.reshape(heads_all), loss.reshape(()))


def solution(mesh):
    in_specs = (
        P("fsdp", "ctx", None),
        P("fsdp", "ctx", None),
        P("fsdp", "ctx", None),
        P("fsdp", None, "ctx"),
        P("fsdp", None),
        P(),
        P(),
    )
    out_specs = (P("fsdp", None), P(), P(), P())
    return jax.shard_map(local, mesh=mesh, in_specs=in_specs, out_specs=out_specs, check_vma=False)
```

time: 369 us -> 117 us (0.32)
  waiting for transfers between devices: 226 us -> 19.8 us
  other arithmetic: 33.2 us -> 0.21 us
  Pallas kernels: 0 us -> 21.7 us
  matrix products: 18.8 us -> 0 us
  local copies, waits for them, and re-layouts: 19.3 us -> 1.33 us
  between operations: 15.3 us -> 0.77 us
  starting transfers between devices: 0.2 us -> 11.1 us
  blocking collectives: 54.6 us -> 61.6 us
    all_gather x3 -> x0, waiting for transfers between devices: 133 us -> none  [the longest x2 85.3 us: prefix(): pieces = jax.tree.map(lambda part: lax.all_gather(part, axis), value)]
    reduce_scatter x1 -> x0, waiting for transfers between devices: 72.8 us -> none  [local(): lax.psum_scatter(lax.dot_general(picked, proj_grad, (((0,), (0,)), ((), (...]
    all_to_all x0 -> x3, blocking collectives: none -> 42.7 us  [the longest x2 25.1 us: exchange(): return lax.all_to_all(blocks, axis, 0, 0, tiled=True)]
    psum x1 -> x0, blocking collectives: 40.8 us -> none  [local(): totals = lax.psum((loss_part, alog_part, skip_part), ('fsdp', 'ctx'))]
    select_n x15 -> x0, other arithmetic: 29.1 us -> none  [the longest x14 29 us: hop(): jnp.where(position < mine, new, old)]
    pallas_call x0 -> x10, Pallas kernels: none -> 21.7 us  [the longest x1 7.29 us: mixer(): pl.pallas_call(functools.partial(mixer_kernel, heads, scale, count), out_...]
    ppermute x0 -> x8, waiting for transfers between devices: none -> 19.8 us  [swap(): lax.ppermute(block, axis, [(i, i ^ shift) for i in range(lax.axis_size(ax...]
    psum x1 -> x0, waiting for transfers between devices: 19 us -> none  [local(): grad_w = lax.psum(shard_grad, 'ctx')]
  transfers between devices with their start and end apart: 5 -> 9, of which waited for: 5 -> 6; matrix products, arithmetic and copies ran while one was open for 4% -> 0% of each run, Pallas kernels for 0% -> 12%
where the time goes in v1:
time: 117 us
  blocking collectives  61.6 us (53%)
  Pallas kernels  21.7 us (19%)
  waiting for transfers between devices  19.8 us (17%)
  starting transfers between devices  11.1 us (9%)
  local copies, waits for them, and re-layouts  1.33 us (1%)
    all_to_all x2, blocking collectives, exchange(): return lax.all_to_all(blocks, axis, 0, 0, tiled=True)  25.1 us
    ppermute x8, waiting for transfers between devices, swap(): lax.ppermute(block, axis, [(i, i ^ shift) for i in range(lax.axis_size(ax...  19.8 us
    all_to_all x1, blocking collectives, local(): lax.all_to_all(grad, 'ctx', 0, 0, tiled=True, axis_index_groups=chips)  17.6 us
    all_gather x1, blocking collectives, local(): maps = lax.all_gather(projection, 'ctx', axis=0, tiled=True)  9.62 us
    all_gather x1, blocking collectives, local(): lax.all_gather(grad, 'ctx', axis=0)  9.28 us
    pallas_call x1, Pallas kernels, mixer(): pl.pallas_call(functools.partial(mixer_kernel, heads, scale, count), out_...  7.29 us
    ppermute x8, starting transfers between devices, swap(): lax.ppermute(block, axis, [(i, i ^ shift) for i in range(lax.axis_size(ax...  5.81 us
    all_to_all x1, starting transfers between devices, exchange(): return lax.all_to_all(blocks, axis, 0, 0, tiled=True)  5.31 us
  transfers between devices with their start and end apart: 9, of which 6 were waited for; matrix products, arithmetic and copies ran while one was open for 0% of the time, Pallas kernels for 12%

profile of v1, /device:TPU:0, one launch (start us, length us, event | category | flops | bytes accessed | tf_op | source)
XLA Modules:
  0.0 116.6 jit_solution(1597788094246889216)
XLA Ops:
  0.6 4.0 %pack_mixer.1 = (bf16[8,1040,128]{2,1,0:T(8,128)(2,1)}, bf16[1024,128]{1,0:T(8,128)(2,1)}) custom-call(s32[1]{0:T(128)} %bitcast.core_ref, bf16[1,128,4096]{2,1,0:T(8,128)(2,1)} %values_hbm.1, bf16[1,128,4096]{2,1,0:T(8,128)(2,1)} %targets_hbm.1, f32[1,32,128]{2,1,0:T(8,128)} %dt_ref.1, bf16[2048,128]{1,0:T(8,128)(2,1)} %refs_0_.1), custom_call_target="tpu_custom_call" | custom-call | tf_op jit(solution)/shard_map/pack_mixer/pallas_call | solution.py:288
  4.7 0.0 copy-start.3
  4.7 0.0 copy-start.4
  4.7 0.0 copy-start
  4.7 5.3 %all-to-all-start = ((bf16[8,1040,128]{2,1,0:T(8,128)(2,1)}), bf16[8,1040,128]{2,1,0:T(8,128)(2,1)}, u32[]{:S(2)}, u32[]{:S(2)}) async-start(bf16[8,1040,128]{2,1,0:T(8,128)(2,1)} %get-tuple-element.36), calls=%async_computation | async-start | bytes 4259840 | tf_op jit(solution)/shard_map/all_to_all | solution.py:460
  10.1 2.3 %collective-permute-start = (bf16[1024,128]{1,0:T(8,128)(2,1)}, bf16[1024,128]{1,0:T(8,128)(2,1)S(1)}, u32[]{:S(2)}, u32[]{:S(2)}) collective-permute-start(bf16[1024,128]{1,0:T(8,128)(2,1)} %get-tuple-element.31), channel_id=1, source_target_pairs={{0,8},{8,0},{16,24},{24,16},{1,9},{9,1},{17,25},{25,17},{2,10},{10... | collective-permute-start | bytes 786440 | tf_op jit(solution)/shard_map/ppermute | solution.py:464
  12.3 2.6 %collective-permute-start.1 = (bf16[1024,128]{1,0:T(8,128)(2,1)}, bf16[1024,128]{1,0:T(8,128)(2,1)S(1)}, u32[]{:S(2)}, u32[]{:S(2)}) collective-permute-start(bf16[1024,128]{1,0:T(8,128)(2,1)} %get-tuple-element.31), channel_id=1, source_target_pairs={{0,16},{8,24},{16,0},{24,8},{1,17},{9,25},{17,1},{25,9},{2,18},{10... | collective-permute-start | bytes 786440 | tf_op jit(solution)/shard_map/ppermute | solution.py:464
  14.9 0.0 collective-permute-start.2
  14.9 0.0 copy-done.3
  14.9 0.1 exponential_negate_fusion
  15.0 0.1 broadcast_in_dim_tile.3
  15.1 0.0 copy-done.4
  15.1 0.1 dynamic_slice.7.skip_ref
  15.2 0.0 copy-done
  15.2 0.1 pack_hidden.1
  15.2 0.0 copy-start.2
  15.3 1.0 copy-done.2
  16.2 0.1 pad_add_fusion.chunk_ref
  16.3 0.0 copy-done.1
  16.3 0.8 project.2.start_ref
  17.1 7.3 %collective-permute-done.refs_0_ = bf16[1024,128]{1,0:T(8,128)(2,1)S(1)} collective-permute-done((bf16[1024,128]{1,0:T(8,128)(2,1)}, bf16[1024,128]{1,0:T(8,128)(2,1)S(1)}, u32[]{:S(2)}, u32[]{:S(2)}) %collective-permute-start) | collective-permute-done | bytes 262176 | tf_op jit(solution)/shard_map/ppermute | solution.py:464
  24.4 9.5 %collective-permute-done.1.refs_2_ = bf16[1024,128]{1,0:T(8,128)(2,1)S(1)} collective-permute-done((bf16[1024,128]{1,0:T(8,128)(2,1)}, bf16[1024,128]{1,0:T(8,128)(2,1)S(1)}, u32[]{:S(2)}, u32[]{:S(2)}) %collective-permute-start.1) | collective-permute-done | bytes 262176 | tf_op jit(solution)/shard_map/ppermute | solution.py:464
  33.9 0.0 collective-permute-done.2.refs_4_
  33.9 0.0 collective-permute-start.3
  33.9 0.5 collective-permute-start.4
  34.4 0.0 collective-permute-start.5
  34.4 0.1 stack.36.chunk_ref
  34.5 0.9 collective-permute-done.3.refs_1_
  35.4 0.5 collective-permute-done.4.refs_3_
  35.9 0.4 collective-permute-done.5.refs_5_
  36.3 1.5 %project.3 = bf16[128,128]{1,0:T(8,128)(2,1)S(1)} custom-call(s32[6]{0:T(128)S(1)} %stack.36.chunk_ref, bf16[1,128,8192]{2,1,0:T(8,128)(2,1)S(1)} %copy-done, f32[128,128]{1,0:T(8,128)S(1)} %project.2.start_ref, bf16[1024,128]{1,0:T(8,128)(2,1)S(1)} %collective-permute-done.refs_0_, bf16[1024,128]{1,0:T(8,128)(2,1)S(1)} %collective-permute-done.3.refs_1_, ...), custom_call_target="tpu_custom_call" | custom-call | tf_op jit(solution)/shard_map/project/pallas_call | solution.py:340
  37.8 0.0 all-to-all-done.vt_ref
  37.8 9.6 %all_gather.9.maps_ref = bf16[1024,128]{1,0:T(8,128)(2,1)S(1)} all-gather(bf16[128,128]{1,0:T(8,128)(2,1)S(1)} %project.3), channel_id=1, replica_groups=mesh['fsdp'=4,'ctx'=8] {'ctx'}, dimensions={0}, use_global_device_ids=true | all-gather | bytes 294912 | tf_op jit(solution)/shard_map/all_gather | solution.py:506
  47.5 0.4 collective-permute-start.7
  47.8 0.1 copy.12.rate_ref
  47.9 4.8 %prepare.1 = (bf16[32,128,128]{2,1,0:T(8,128)(2,1)S(1)}, f32[32,128,128]{2,1,0:T(8,128)S(1)}, f32[32,128,128]{2,1,0:T(8,128)S(1)}, f32[32,128,128]{2,1,0:T(8,128...) custom-call(bf16[8,1040,128]{2,1,0:T(8,128)(2,1)} %all-to-all-done.v, ...), custom_call_target="tpu_custom_call" | custom-call | tf_op jit(solution)/shard_map/prepare/pallas_call | solution.py:201
  52.7 7.3 %mixer.1 = (bf16[1024,128]{1,0:T(8,128)(2,1)S(1)}, bf16[16,128]{1,0:T(8,128)(2,1)S(1)}) custom-call(bf16[1024,128]{1,0:T(8,128)(2,1)S(1)} %all_gather.9.maps_ref, bf16[32,128,128]{2,1,0:T(8,128)(2,1)S(1)} %get-tuple-element.43.v_ref, f32[32,128,128]{2,1,0:T(8,128)S(1)} %get-tuple-element.44.within_ref, f32[32,128,128]{2,1,0:T(8,128)S(1)} %get-tuple-element.45.sloped_ref, ...), custom_call_target="tpu_custom_call" | custom-call | flops 939524096 | bytes 3145728 | tf_op jit(solution)/shard_map/mixer/pallas_call | solution.py:227
  60.0 9.5 %all_to_all.20 = bf16[8,128,128]{2,1,0:T(8,128)(2,1)S(1)} all-to-all(bf16[8,128,128]{2,1,0:T(8,128)(2,1)S(1)} %bitcast.18), channel_id=1, replica_groups=mesh['fsdp'=4,'ctx'=8] {'ctx'}, dimensions={0} | all-to-all | bytes 524288 | tf_op jit(solution)/shard_map/all_to_all | solution.py:460
  69.6 0.1 collective-permute-start.6
  69.6 1.2 %collective-permute-done.6.far_ref = bf16[272,128]{1,0:T(8,128)(2,1)S(1)} collective-permute-done((bf16[272,128]{1,0:T(8,128)(2,1)S(1)}, bf16[272,128]{1,0:T(8,128)(2,1)S(1)}, u32[]{:S(2)}, u32[]{:S(2)}) %collective-permute-start.6) | collective-permute-done | bytes 69664 | tf_op jit(solution)/shard_map/ppermute | solution.py:464
  70.9 0.0 collective-permute-done.7.feats_ref
  70.9 1.3 %weight_grad.1 = bf16[4,1040,128]{2,1,0:T(8,128)(2,1)S(1)} custom-call(s32[1]{0:T(128)} %bitcast.core_ref, bf16[272,128]{1,0:T(8,128)(2,1)S(1)} %pad_maximum_fusion.near_ref, bf16[272,128]{1,0:T(8,128)(2,1)S(1)} %collective-permute-done.6.far_ref, bf16[1,128,8192]{2,1,0:T(8,128)(2,1)S(1)} %copy-done, bf16[128,4096]{1,0:T(8,128)(2,1)S(1)} %collective-permute-done.7.feats_ref), custom_call_target="tpu_custom_call" | custom-call | tf_op jit(solution)/shard_map/weight_grad/pallas_call | solution.py:383
  72.2 17.6 %all_to_all.21.grad_ref = bf16[4,1040,128]{2,1,0:T(8,128)(2,1)S(1)} all-to-all(bf16[4,1040,128]{2,1,0:T(8,128)(2,1)S(1)} %weight_grad.1), channel_id=1, replica_groups={{0,2,4,6},{1,3,5,7},{8,10,12,14},{9,11,13,15},{16,18,20,22},{17,19,21,2..., dimensions={0} | all-to-all | bytes 2129920 | tf_op jit(solution)/shard_map/all_to_all | solution.py:522
  89.9 0.2 add_chips.1
  90.1 15.6 %all_to_all.22.grad_ref = bf16[4,272,128]{2,1,0:T(8,128)(2,1)S(1)} all-to-all(bf16[4,272,128]{2,1,0:T(8,128)(2,1)S(1)} %add_chips.1), channel_id=1, replica_groups=mesh['fsdp'=4,'ctx'=8] {'fsdp'}, dimensions={0} | all-to-all | bytes 557056 | tf_op jit(solution)/shard_map/all_to_all | solution.py:460
  105.6 0.6 add_blocks.1
  106.2 9.3 %all-gather = bf16[2048,128]{1,0:T(8,128)(2,1)S(1)} all-gather(bf16[256,128]{1,0:T(8,128)(2,1)S(1)} %get-tuple-element.54), channel_id=2, replica_groups=mesh['fsdp'=4,'ctx'=8] {'ctx'}, dimensions={0}, use_global_device_ids=true | all-gather | bytes 589824 | tf_op jit(solution)/shard_map/all_gather | solution.py:525
  115.5 1.0 finish.1
  (6 shorter events, 0.1 us)
Async XLA Ops:
  4.7 10.2 %copy-start.3 = (f32[32]{0:T(128)S(1)}, f32[32]{0:T(128)}, u32[]{:S(2)}) copy-start(f32[32]{0:T(128)} %param.12) | copy-start | bytes 388
  4.7 10.4 %copy-start.4 = (f32[32]{0:T(128)S(1)}, f32[32]{0:T(128)}, u32[]{:S(2)}) copy-start(f32[32]{0:T(128)} %param.13) | copy-start | bytes 388
  4.7 10.4 %copy-start = (bf16[1,128,8192]{2,1,0:T(8,128)(2,1)S(1)}, bf16[1,128,8192]{2,1,0:T(8,128)(2,1)}, u32[]{:S(2)}) copy-start(bf16[1,128,8192]{2,1,0:T(8,128)(2,1)} %hidden_ref.7) | copy-start | bytes 6291460
  4.7 33.1 %all-to-all-start = ((bf16[8,1040,128]{2,1,0:T(8,128)(2,1)}), bf16[8,1040,128]{2,1,0:T(8,128)(2,1)}, u32[]{:S(2)}, u32[]{:S(2)}) async-start(bf16[8,1040,128]{2,1,0:T(8,128)(2,1)} %get-tuple-element.36), calls=%async_computation | async-start | bytes 4259840 | tf_op jit(solution)/shard_map/all_to_all | solution.py:460
  10.0 6.3 %copy-start.1 = (bf16[2048,128]{1,0:T(8,128)(2,1)S(1)}, bf16[2048,128]{1,0:T(8,128)(2,1)}, u32[]{:S(2)}) copy-start(bf16[2048,128]{1,0:T(8,128)(2,1)} %refs_0_.1) | copy-start | bytes 1572868
  10.1 14.3 %collective-permute-start = (bf16[1024,128]{1,0:T(8,128)(2,1)}, bf16[1024,128]{1,0:T(8,128)(2,1)S(1)}, u32[]{:S(2)}, u32[]{:S(2)}) collective-permute-start(bf16[1024,128]{1,0:T(8,128)(2,1)} %get-tuple-element.31), channel_id=1, source_target_pairs={{0,8},{8,0},{16,24},{24,16},{1,9},{9,1},{17,25},{25,17},{2,10},{10... | collective-permute-start | bytes 786440 | tf_op jit(solution)/shard_map/ppermute | solution.py:464
  12.3 21.6 %collective-permute-start.1 = (bf16[1024,128]{1,0:T(8,128)(2,1)}, bf16[1024,128]{1,0:T(8,128)(2,1)S(1)}, u32[]{:S(2)}, u32[]{:S(2)}) collective-permute-start(bf16[1024,128]{1,0:T(8,128)(2,1)} %get-tuple-element.31), channel_id=1, source_target_pairs={{0,16},{8,24},{16,0},{24,8},{1,17},{9,25},{17,1},{25,9},{2,18},{10... | collective-permute-start | bytes 786440 | tf_op jit(solution)/shard_map/ppermute | solution.py:464
  14.9 19.0 %collective-permute-start.2 = (bf16[1024,128]{1,0:T(8,128)(2,1)}, bf16[1024,128]{1,0:T(8,128)(2,1)S(1)}, u32[]{:S(2)}, u32[]{:S(2)}) collective-permute-start(bf16[1024,128]{1,0:T(8,128)(2,1)} %get-tuple-element.31), channel_id=1, source_target_pairs={{0,24},{8,16},{16,8},{24,0},{1,25},{9,17},{17,9},{25,1},{2,26},{10... | collective-permute-start | bytes 786440 | tf_op jit(solution)/shard_map/ppermute | solution.py:464
  15.2 1.0 copy-start.2
  33.9 1.5 %collective-permute-start.3 = (bf16[1024,128]{1,0:T(8,128)(2,1)S(1)}, bf16[1024,128]{1,0:T(8,128)(2,1)S(1)}, u32[]{:S(2)}, u32[]{:S(2)}) collective-permute-start(bf16[1024,128]{1,0:T(8,128)(2,1)S(1)} %collective-permute-done.refs_0_), channel_id=1, source_target_pairs={{0,1},{1,0},{2,3},{3,2},{4,5},{5,4},{6,7},{7,6},{8,9},{9,8},{10,11... | collective-permute-start | bytes 786440 | tf_op jit(solution)/shard_map/ppermute | solution.py:464
  33.9 2.0 %collective-permute-start.4 = (bf16[1024,128]{1,0:T(8,128)(2,1)S(1)}, bf16[1024,128]{1,0:T(8,128)(2,1)S(1)}, u32[]{:S(2)}, u32[]{:S(2)}) collective-permute-start(bf16[1024,128]{1,0:T(8,128)(2,1)S(1)} %collective-permute-done.1.refs_2_), channel_id=1, source_target_pairs={{0,1},{1,0},{2,3},{3,2},{4,5},{5,4},{6,7},{7,6},{8,9},{9,8},{10,11... | collective-permute-start | bytes 786440 | tf_op jit(solution)/shard_map/ppermute | solution.py:464
  34.4 1.9 %collective-permute-start.5 = (bf16[1024,128]{1,0:T(8,128)(2,1)S(1)}, bf16[1024,128]{1,0:T(8,128)(2,1)}, u32[]{:S(2)}, u32[]{:S(2)}) collective-permute-start(bf16[1024,128]{1,0:T(8,128)(2,1)S(1)} %collective-permute-done.2.refs_4_), channel_id=1, source_target_pairs={{0,1},{1,0},{2,3},{3,2},{4,5},{5,4},{6,7},{7,6},{8,9},{9,8},{10,11... | collective-permute-start | bytes 786440 | tf_op jit(solution)/shard_map/ppermute | solution.py:464
  47.5 23.4 %collective-permute-start.7 = (bf16[128,4096]{1,0:T(8,128)(2,1)}, bf16[128,4096]{1,0:T(8,128)(2,1)S(1)}, u32[]{:S(2)}, u32[]{:S(2)}) collective-permute-start(bf16[128,4096]{1,0:T(8,128)(2,1)} %copy-done.2), channel_id=1, source_target_pairs={{0,1},{1,0},{2,3},{3,2},{4,5},{5,4},{6,7},{7,6},{8,9},{9,8},{10,11... | collective-permute-start | bytes 3145736 | tf_op jit(solution)/shard_map/ppermute | solution.py:464
  69.6 1.3 %collective-permute-start.6 = (bf16[272,128]{1,0:T(8,128)(2,1)S(1)}, bf16[272,128]{1,0:T(8,128)(2,1)S(1)}, u32[]{:S(2)}, u32[]{:S(2)}) collective-permute-start(bf16[272,128]{1,0:T(8,128)(2,1)S(1)} %pad_maximum_fusion.near_ref), channel_id=1, source_target_pairs={{0,1},{1,0},{2,3},{3,2},{4,5},{5,4},{6,7},{7,6},{8,9},{9,8},{10,11... | collective-permute-start | bytes 208904 | tf_op jit(solution)/shard_map/ppermute | solution.py:464

commit v2 on v1

--- a/solution.py
+++ b/solution.py
@@ -43,100 +43,93 @@
     return jnp.maximum(value, 0.0) + jnp.where(small < 0.03, series, jnp.log1p(small))
 
 
-def prepare_kernel(
-    heads, vt_ref, rate_ref, skip_ref, v_ref, within_ref, sloped_ref, base_ref, weighed_ref,
-    cols_ref, carry_ref, last_ref, rows_ref,
+def mixer_kernel(
+    heads, scale, count, maps_ref, vt_hbm, rate_ref, skip_ref, first_ref, out_ref, pack_ref,
+    vt_ref, rows_ref, cols_ref, carry_ref, last_ref, states, entries, parts, stat_ref, sems,
 ):
     blocks, tail_at, width = vt_ref.shape[0], vt_ref.shape[1] - PAD, vt_ref.shape[2]
+    half = maps_ref.shape[1] // 2
+    full = heads * width
+    tail = pltpu.make_async_copy(
+        vt_hbm.at[:, pl.ds(tail_at, PAD)], vt_ref.at[:, pl.ds(tail_at, PAD)], sems.at[blocks]
+    )
+    tail.start()
+
+    def load(k):
+        body = pl.ds(0, tail_at)
+        return pltpu.make_async_copy(vt_hbm.at[k, body], vt_ref.at[k, body], sems.at[k])
+
+    for k in range(blocks):
+        load(k).start()
+    stat_ref[...] = jnp.zeros_like(stat_ref)
     t_at = lax.broadcasted_iota(jnp.int32, (BLOCK, BLOCK), 0)
     s_at = lax.broadcasted_iota(jnp.int32, (BLOCK, BLOCK), 1)
     mask = t_at >= s_at
+    tail.wait()
     sent = []
     for k in range(blocks):
         rows = vt_ref[k, tail_at:, :].astype(jnp.float32)
         sent.append(rows[:heads] + rows[heads : 2 * heads] + rows[2 * heads : 3 * heads])
     step = softplus(jnp.concatenate(sent, axis=0))
     decay = running_sum(step * rate_ref[...])
-    decay_c, step_c = decay.T, step.T
-    tail_c = decay_c[BLOCK - 1 :, :] - decay_c
-    growth_c = jnp.exp(decay_c)
-    end_c = jnp.exp(tail_c) * step_c
-    rise_c = growth_c * decay_c
-
-    def spread(row):
-        each = [jnp.broadcast_to(row[:, h : h + 1], (1, width)) for h in range(heads)]
-        return jnp.concatenate(each, axis=1)
-
+    final = decay[:, BLOCK - 1 :]
+    growth = jnp.exp(decay)
+    tails = final - decay
+    made = (growth, growth * decay, jnp.exp(tails) * step, tails, decay, step)
+    carry = jnp.broadcast_to(jnp.exp(final), (blocks * heads, width))
+    last = jnp.broadcast_to(jnp.exp(final) * final, (blocks * heads, width))
     for k in range(blocks):
         own = slice(k * heads, (k + 1) * heads)
-        made = (growth_c, rise_c, end_c, tail_c, decay_c)
-        cols_ref[k] = jnp.concatenate([x[:, own] for x in made], axis=1)
-        rows_ref[k, :heads, :] = decay[own, :]
-        rows_ref[k, heads:, :] = step[own, :]
-        carry_ref[k] = spread(growth_c[BLOCK - 1 :, own])
-        last_ref[k] = spread(rise_c[BLOCK - 1 :, own])
-
-    def block(k, carry):
-        cols, rows = cols_ref[k], rows_ref[k]
+        rows_ref[k] = jnp.concatenate([x[own, :] for x in made], axis=0)
         for h in range(heads):
-            i = k * heads + h
-            col = lambda j: cols[:, j * heads + h : j * heads + h + 1]
-            diff = jnp.minimum(col(4) - rows[h : h + 1, :], 0.0)
-            within = jnp.where(mask, jnp.exp(diff), 0.0) * rows[heads + h : heads + h + 1, :]
-            within_ref[i] = within
-            sloped_ref[i] = within * diff
-            v = vt_ref[k, h * BLOCK : (h + 1) * BLOCK, :]
-            goal = vt_ref[k, (heads + h) * BLOCK : (heads + h + 1) * BLOCK, :]
-            vf = v.astype(jnp.float32)
-            v_ref[i] = v
-            base_ref[i] = skip_ref[h] * vf - goal.astype(jnp.float32)
-            weighed_ref[k, :, h * width : (h + 1) * width] = (vf * col(2)).astype(jnp.bfloat16)
-        return carry
-
-    lax.fori_loop(0, blocks, block, 0)
-
-
-def mixer_kernel(
-    heads, scale, count, maps_ref, v_ref, within_ref, sloped_ref, base_ref, weighed_ref, cols_ref,
-    carry_ref, last_ref, first_ref, out_ref, pack_ref, states, entries, parts, stat_ref,
-):
-    blocks, width = cols_ref.shape[0], v_ref.shape[2]
-    half = maps_ref.shape[1] // 2
-    full = heads * width
-    stat_ref[...] = jnp.zeros_like(stat_ref)
+            one = slice(k * heads + h, k * heads + h + 1)
+            carry_ref[k, :, h * width : (h + 1) * width] = carry[one, :]
+            last_ref[k, :, h * width : (h + 1) * width] = last[one, :]
 
     def forward(k, state):
+        load(k).wait()
         at = pl.ds(pl.multiple_of(k * BLOCK, BLOCK), BLOCK)
-        maps, cols = maps_ref[at, :], cols_ref[k]
+        maps, rows = maps_ref[at, :], rows_ref[k]
+        cols = rows.T
+        cols_ref[k] = cols
         b, c = maps[:, :half], maps[:, half:]
         scores = dot(c, b, ((1,), (1,)))
         state_bf = state.astype(jnp.bfloat16)
         states[k] = state
         from_all = dot(c, state_bf, ((1,), (0,)))
         score_grad = jnp.zeros((BLOCK, BLOCK), jnp.float32)
-        grown = []
+        grown, weighed = [], []
         for h in range(heads):
-            i = k * heads + h
-            v, within = v_ref[i], within_ref[i]
-            growth, rise = cols[:, h : h + 1], cols[:, heads + h : heads + h + 1]
-            inner = dot((within * scores).astype(jnp.bfloat16), v, ((1,), (0,)))
+            col = lambda j: cols[:, j * heads + h : j * heads + h + 1]
+            v = vt_ref[k, h * BLOCK : (h + 1) * BLOCK, :]
+            goal = vt_ref[k, (heads + h) * BLOCK : (heads + h + 1) * BLOCK, :]
+            vf = v.astype(jnp.float32)
+            row = lambda j: rows[j * heads + h : j * heads + h + 1, :]
+            diff = jnp.minimum(col(4) - row(4), 0.0)
+            within = jnp.where(mask, jnp.exp(diff), 0.0) * row(5)
+            mixing = within * scores
+            inner = dot(mixing.astype(jnp.bfloat16), v, ((1,), (0,)))
             from_state = from_all[:, h * width : (h + 1) * width]
-            misfit = inner + growth * from_state + base_ref[i]
+            growth = col(0)
+            out = inner + growth * from_state + skip_ref[h] * vf
+            misfit = out - goal.astype(jnp.float32)
             grad = misfit * scale
             mix_grad = dot(grad.astype(jnp.bfloat16), v, ((1,), (1,)))
             grown.append((grad * growth).astype(jnp.bfloat16))
+            weighed.append((vf * col(2)).astype(jnp.bfloat16))
             stat_ref[h, 0] += fold(misfit * misfit)
-            stat_ref[h, 1] += fold(grad * v.astype(jnp.float32))
-            stat_ref[h, 2] += fold(grad * from_state * rise)
+            stat_ref[h, 1] += fold(grad * vf)
+            stat_ref[h, 2] += fold(grad * from_state * col(1))
             score_grad += within * mix_grad
-            stat_ref[h, 2] += fold(mix_grad * scores * sloped_ref[i])
+            stat_ref[h, 2] += fold(mix_grad * mixing * diff)
         grown = jnp.concatenate(grown, axis=1)
+        weighed = jnp.concatenate(weighed, axis=1)
         entries[k] = dot(c, grown, ((0,), (0,)))
         score_bf = score_grad.astype(jnp.bfloat16)
         grad_c = dot(grown, state_bf, ((1,), (1,))) + dot(score_bf, b, ((1,), (0,)))
         grad_b = dot(score_bf, c, ((0,), (0,)))
         parts[at, :] = jnp.concatenate([grad_b, grad_c], axis=1)
-        return carry_ref[k] * state + dot(b, weighed_ref[k], ((0,), (0,)))
+        return carry_ref[k] * state + dot(b, weighed, ((0,), (0,)))
 
     unrolled(blocks, forward, jnp.zeros((half, full), jnp.float32))
 
@@ -150,11 +143,12 @@
         overlap = leaving * states[k] * last_ref[k]
         for h in range(heads):
             piece = slice(h * width, (h + 1) * width)
-            coef_grad = dot(v_ref[k * heads + h], leaving_bf[:, piece], ((1,), (1,)))
+            v = vt_ref[k, h * BLOCK : (h + 1) * BLOCK, :]
+            coef_grad = dot(v, leaving_bf[:, piece], ((1,), (1,)))
             pulled = coef_grad * cols[:, 2 * heads + h : 2 * heads + h + 1]
             grad_b += pulled
-            tail = cols[:, 3 * heads + h : 3 * heads + h + 1]
-            stat_ref[h, 2, :, :half] += fold(pulled * bf * tail)
+            tail_w = cols[:, 3 * heads + h : 3 * heads + h + 1]
+            stat_ref[h, 2, :, :half] += fold(pulled * bf * tail_w)
             stat_ref[h, 2] += fold(overlap[:, piece])
         both = jnp.concatenate([grad_b, jnp.zeros_like(grad_b)], axis=1)
         out_ref[at, :] = (parts[at, :] + both).astype(out_ref.dtype)
@@ -192,37 +186,10 @@
 LIMIT = 28 * 1024 * 1024
 
 
-def prepare(vt, rates, skip):
+def mixer(maps, vt, rates, skip, first, scale, count):
     blocks, rows, width = vt.shape
+    length, both = maps.shape
     heads = (rows - PAD) // BLOCK // 2
-    units, full = blocks * heads, heads * width
-    square = jax.ShapeDtypeStruct((units, BLOCK, BLOCK), jnp.float32)
-    row = jax.ShapeDtypeStruct((blocks, 1, full), jnp.float32)
-    return pl.pallas_call(
-        functools.partial(prepare_kernel, heads),
-        out_shape=(
-            jax.ShapeDtypeStruct((units, BLOCK, width), jnp.bfloat16),
-            square,
-            square,
-            jax.ShapeDtypeStruct((units, BLOCK, width), jnp.float32),
-            jax.ShapeDtypeStruct((blocks, BLOCK, full), jnp.bfloat16),
-            jax.ShapeDtypeStruct((blocks, BLOCK, 5 * heads), jnp.float32),
-            row,
-            row,
-        ),
-        in_specs=[VMEM, VMEM, SMEM],
-        out_specs=(VMEM,) * 8,
-        scratch_shapes=[pltpu.VMEM((blocks, 2 * heads, BLOCK), jnp.float32)],
-        compiler_params=pltpu.CompilerParams(vmem_limit_bytes=LIMIT),
-        name="prepare",
-    )(vt, rates, skip)
-
-
-def mixer(maps, ready, first, scale, count):
-    length, both = maps.shape
-    units, _, width = ready[0].shape
-    blocks = length // BLOCK
-    heads = units // blocks
     full = heads * width
     return pl.pallas_call(
         functools.partial(mixer_kernel, heads, scale, count),
@@ -230,20 +197,26 @@
             jax.ShapeDtypeStruct((length, both), jnp.bfloat16),
             jax.ShapeDtypeStruct((PAD, 128), jnp.bfloat16),
         ),
-        in_specs=[VMEM] * 9 + [SMEM],
+        in_specs=[VMEM, ANY, VMEM, SMEM, SMEM],
         out_specs=(VMEM, VMEM),
         scratch_shapes=[
+            pltpu.VMEM((blocks, rows, width), jnp.bfloat16),
+            pltpu.VMEM((blocks, 6 * heads, BLOCK), jnp.float32),
+            pltpu.VMEM((blocks, BLOCK, 6 * heads), jnp.float32),
+            pltpu.VMEM((blocks, 1, full), jnp.float32),
+            pltpu.VMEM((blocks, 1, full), jnp.float32),
             pltpu.VMEM((blocks, both // 2, full), jnp.float32),
             pltpu.VMEM((blocks, both // 2, full), jnp.float32),
             pltpu.VMEM((length, both), jnp.float32),
             pltpu.VMEM((heads, 3, 8, 128), jnp.float32),
+            pltpu.SemaphoreType.DMA((blocks + 1,)),
         ],
         compiler_params=pltpu.CompilerParams(vmem_limit_bytes=LIMIT),
         cost_estimate=pl.CostEstimate(
             flops=14 * length * BLOCK * full, bytes_accessed=6 * length * full, transcendentals=0
         ),
         name="mixer",
-    )(maps, *ready, first.reshape(1))
+    )(maps, vt, rates, skip, first.reshape(1))
 
 
 def pack_mixer_kernel(
@@ -492,10 +465,8 @@
     send = pack_hidden(1 - core, hidden, half)
     start = jnp.zeros((rows, both), jnp.float32)
     start = project([2 * shard, 2 * shard + 1], hidden, [proj_weight], start, jnp.float32)
-    near, send, rates, s_mine, start = lax.optimization_barrier(
-        (near, send, rates, s_mine, start)
-    )
     far = [swap(block, "ctx", 1) for block in near]
+    far, send, rates, s_mine, start = lax.optimization_barrier((far, send, rates, s_mine, start))
 
     near_at = [2 * other + core for other in others]
     far_at = [2 * other + 1 - core for other in others]
@@ -507,8 +478,7 @@
     maps, send = lax.optimization_barrier((maps, send))
     feats = swap(send, "ctx", 1)
 
-    ready = prepare(vt, rates, s_mine)
-    proj_part, packed = mixer(maps, ready, first, scale, heads_all)
+    proj_part, packed = mixer(maps, vt, rates, s_mine, first, scale, heads_all)
 
     proj_part = exchange(proj_part.reshape(ctx, rows, both), "ctx").astype(jnp.float32)
     proj_grad = jnp.sum(proj_part, axis=0)

time: 117 us -> 116 us (level)
    pallas_call x1 -> x0, Pallas kernels: 4.79 us -> none  [prepare(): pl.pallas_call(functools.partial(prepare_kernel, heads), out_shape=(jax.S...]
    pallas_call x1, Pallas kernels: 7.29 us -> 10.9 us  [mixer(): pl.pallas_call(functools.partial(mixer_kernel, heads, scale, count), out_...]
  transfers between devices with their start and end apart: 9 -> 9, of which waited for: 6 -> 3; matrix products, arithmetic and copies ran while one was open for 0% -> 0% of each run, Pallas kernels for 12% -> 12%
where the time goes in v2:
time: 116 us; the launch traced here: 115 us
  blocking collectives  61.1 us (53%)
  Pallas kernels  20.7 us (18%)
  waiting for transfers between devices  20.2 us (17%)
  starting transfers between devices  11.1 us (10%)
  local copies, waits for them, and re-layouts  1.33 us (1%)
    all_to_all x2, blocking collectives, exchange(): return lax.all_to_all(blocks, axis, 0, 0, tiled=True)  24.6 us
    ppermute x8, waiting for transfers between devices, swap(): lax.ppermute(block, axis, [(i, i ^ shift) for i in range(lax.axis_size(ax...  20.2 us
    all_to_all x1, blocking collectives, local(): lax.all_to_all(grad, 'ctx', 0, 0, tiled=True, axis_index_groups=chips)  17.6 us
    pallas_call x1, Pallas kernels, mixer(): pl.pallas_call(functools.partial(mixer_kernel, heads, scale, count), out_...  10.9 us
    all_gather x1, blocking collectives, local(): maps = lax.all_gather(projection, 'ctx', axis=0, tiled=True)  9.62 us
    all_gather x1, blocking collectives, local(): lax.all_gather(grad, 'ctx', axis=0)  9.28 us
    ppermute x8, starting transfers between devices, swap(): lax.ppermute(block, axis, [(i, i ^ shift) for i in range(lax.axis_size(ax...  5.81 us
    all_to_all x1, starting transfers between devices, exchange(): return lax.all_to_all(blocks, axis, 0, 0, tiled=True)  5.31 us
  transfers between devices with their start and end apart: 9, of which 3 were waited for; matrix products, arithmetic and copies ran while one was open for 0% of the time, Pallas kernels for 12%

profile of v2, /device:TPU:0, one launch (start us, length us, event | category | flops | bytes accessed | tf_op | source)
XLA Modules:
  0.0 115.5 jit_solution(8131638100524338041)
XLA Ops:
  0.6 4.0 %pack_mixer.1 = (bf16[8,1040,128]{2,1,0:T(8,128)(2,1)}, bf16[1024,128]{1,0:T(8,128)(2,1)}) custom-call(s32[1]{0:T(128)} %bitcast.core_ref, bf16[1,128,4096]{2,1,0:T(8,128)(2,1)} %values_hbm.1, bf16[1,128,4096]{2,1,0:T(8,128)(2,1)} %targets_hbm.1, f32[1,32,128]{2,1,0:T(8,128)} %dt_ref.1, bf16[2048,128]{1,0:T(8,128)(2,1)} %refs_0_.1), custom_call_target="tpu_custom_call" | custom-call | tf_op jit(solution)/shard_map/pack_mixer/pallas_call | solution.py:261
  4.7 0.0 copy-start.3
  4.7 0.0 copy-start.4
  4.7 0.0 copy-start
  4.7 5.3 %all-to-all-start = ((bf16[8,1040,128]{2,1,0:T(8,128)(2,1)}), bf16[8,1040,128]{2,1,0:T(8,128)(2,1)}, u32[]{:S(2)}, u32[]{:S(2)}) async-start(bf16[8,1040,128]{2,1,0:T(8,128)(2,1)} %get-tuple-element.28), calls=%async_computation | async-start | bytes 4259840 | tf_op jit(solution)/shard_map/all_to_all | solution.py:433
  10.0 0.0 copy-start.1
  10.0 2.3 %collective-permute-start = (bf16[1024,128]{1,0:T(8,128)(2,1)}, bf16[1024,128]{1,0:T(8,128)(2,1)S(1)}, u32[]{:S(2)}, u32[]{:S(2)}) collective-permute-start(bf16[1024,128]{1,0:T(8,128)(2,1)} %get-tuple-element.23), channel_id=1, source_target_pairs={{0,8},{8,0},{16,24},{24,16},{1,9},{9,1},{17,25},{25,17},{2,10},{10... | collective-permute-start | bytes 786440 | tf_op jit(solution)/shard_map/ppermute | solution.py:437
  12.3 2.6 %collective-permute-start.2 = (bf16[1024,128]{1,0:T(8,128)(2,1)}, bf16[1024,128]{1,0:T(8,128)(2,1)S(1)}, u32[]{:S(2)}, u32[]{:S(2)}) collective-permute-start(bf16[1024,128]{1,0:T(8,128)(2,1)} %get-tuple-element.23), channel_id=1, source_target_pairs={{0,16},{8,24},{16,0},{24,8},{1,17},{9,25},{17,1},{25,9},{2,18},{10... | collective-permute-start | bytes 786440 | tf_op jit(solution)/shard_map/ppermute | solution.py:437
  14.9 0.0 collective-permute-start.4
  14.9 9.5 %collective-permute-done.refs_0_ = bf16[1024,128]{1,0:T(8,128)(2,1)S(1)} collective-permute-done((bf16[1024,128]{1,0:T(8,128)(2,1)}, bf16[1024,128]{1,0:T(8,128)(2,1)S(1)}, u32[]{:S(2)}, u32[]{:S(2)}) %collective-permute-start) | collective-permute-done | bytes 262176 | tf_op jit(solution)/shard_map/ppermute | solution.py:437
  24.4 0.0 collective-permute-start.1
  24.4 9.5 %collective-permute-done.2.refs_2_ = bf16[1024,128]{1,0:T(8,128)(2,1)S(1)} collective-permute-done((bf16[1024,128]{1,0:T(8,128)(2,1)}, bf16[1024,128]{1,0:T(8,128)(2,1)S(1)}, u32[]{:S(2)}, u32[]{:S(2)}) %collective-permute-start.2) | collective-permute-done | bytes 262176 | tf_op jit(solution)/shard_map/ppermute | solution.py:437
  33.9 0.0 collective-permute-start.3
  33.9 0.0 collective-permute-done.4.refs_4_
  33.9 0.5 collective-permute-start.5
  34.4 0.0 copy-done.3
  34.4 0.1 exponential_negate_fusion
  34.5 0.1 broadcast_in_dim_tile.3
  34.6 0.0 copy-done.4
  34.6 0.1 dynamic_slice.7.skip_ref
  34.6 0.0 copy-done
  34.6 0.1 pack_hidden.1
  34.7 0.0 copy-start.2
  34.7 1.0 copy-done.2
  35.7 0.1 pad_add_fusion.chunk_ref
  35.8 0.0 copy-done.1
  35.8 0.8 project.2.start_ref
  36.6 0.1 stack.36.chunk_ref
  36.7 0.0 collective-permute-done.1.refs_1_
  36.7 0.0 collective-permute-done.3.refs_3_
  36.7 0.0 collective-permute-done.5.refs_5_
  36.7 1.7 %project.3 = bf16[128,128]{1,0:T(8,128)(2,1)S(1)} custom-call(s32[6]{0:T(128)S(1)} %stack.36.chunk_ref, bf16[1,128,8192]{2,1,0:T(8,128)(2,1)S(1)} %copy-done, f32[128,128]{1,0:T(8,128)S(1)} %project.2.start_ref, bf16[1024,128]{1,0:T(8,128)(2,1)S(1)} %collective-permute-done.refs_0_, bf16[1024,128]{1,0:T(8,128)(2,1)} %collective-permute-done.1.refs_1_, ...), custom_call_target="tpu_custom_call" | custom-call | tf_op jit(solution)/shard_map/project/pallas_call | solution.py:313
  38.4 0.0 all-to-all-done.vt_hbm
  38.4 9.6 %all_gather.9.maps_ref = bf16[1024,128]{1,0:T(8,128)(2,1)S(1)} all-gather(bf16[128,128]{1,0:T(8,128)(2,1)S(1)} %project.3), channel_id=1, replica_groups=mesh['fsdp'=4,'ctx'=8] {'ctx'}, dimensions={0}, use_global_device_ids=true | all-gather | bytes 294912 | tf_op jit(solution)/shard_map/all_gather | solution.py:477
  48.0 0.4 collective-permute-start.7
  48.4 0.1 copy.12.rate_ref
  48.5 10.9 %mixer.1 = (bf16[1024,128]{1,0:T(8,128)(2,1)S(1)}, bf16[16,128]{1,0:T(8,128)(2,1)S(1)}) custom-call(bf16[1024,128]{1,0:T(8,128)(2,1)S(1)} %all_gather.9.maps_ref, bf16[8,1040,128]{2,1,0:T(8,128)(2,1)} %all-to-all-done.vt_hbm, f32[32,1]{1,0:T(8,128)S(1)} %copy.12.rate_ref, f32[4]{0:T(128)S(1)} %dynamic_slice.7.skip_ref, s32[1]{0:T(128)} %bitcast.10.first_ref), custom_call_target="tpu_custom_call" | custom-call | flops 939524096 | bytes 3145728 | tf_op jit(solution)/shard_map/mixer/pallas_call | solution.py:194
  59.4 9.5 %all_to_all.20 = bf16[8,128,128]{2,1,0:T(8,128)(2,1)S(1)} all-to-all(bf16[8,128,128]{2,1,0:T(8,128)(2,1)S(1)} %bitcast.18), channel_id=1, replica_groups=mesh['fsdp'=4,'ctx'=8] {'ctx'}, dimensions={0} | all-to-all | bytes 524288 | tf_op jit(solution)/shard_map/all_to_all | solution.py:433
  69.0 0.1 collective-permute-start.6
  69.1 1.2 %collective-permute-done.6.far_ref = bf16[272,128]{1,0:T(8,128)(2,1)S(1)} collective-permute-done((bf16[272,128]{1,0:T(8,128)(2,1)S(1)}, bf16[272,128]{1,0:T(8,128)(2,1)S(1)}, u32[]{:S(2)}, u32[]{:S(2)}) %collective-permute-start.6) | collective-permute-done | bytes 69664 | tf_op jit(solution)/shard_map/ppermute | solution.py:437
  70.3 0.0 collective-permute-done.7.feats_ref
  70.3 1.3 %weight_grad.1 = bf16[4,1040,128]{2,1,0:T(8,128)(2,1)S(1)} custom-call(s32[1]{0:T(128)} %bitcast.core_ref, bf16[272,128]{1,0:T(8,128)(2,1)S(1)} %pad_maximum_fusion.near_ref, bf16[272,128]{1,0:T(8,128)(2,1)S(1)} %collective-permute-done.6.far_ref, bf16[1,128,8192]{2,1,0:T(8,128)(2,1)S(1)} %copy-done, bf16[128,4096]{1,0:T(8,128)(2,1)S(1)} %collective-permute-done.7.feats_ref), custom_call_target="tpu_custom_call" | custom-call | tf_op jit(solution)/shard_map/weight_grad/pallas_call | solution.py:356
  71.7 17.6 %all_to_all.21.grad_ref = bf16[4,1040,128]{2,1,0:T(8,128)(2,1)S(1)} all-to-all(bf16[4,1040,128]{2,1,0:T(8,128)(2,1)S(1)} %weight_grad.1), channel_id=1, replica_groups={{0,2,4,6},{1,3,5,7},{8,10,12,14},{9,11,13,15},{16,18,20,22},{17,19,21,2..., dimensions={0} | all-to-all | bytes 2129920 | tf_op jit(solution)/shard_map/all_to_all | solution.py:492
  89.3 0.2 add_chips.1
  89.5 15.1 %all_to_all.22.grad_ref = bf16[4,272,128]{2,1,0:T(8,128)(2,1)S(1)} all-to-all(bf16[4,272,128]{2,1,0:T(8,128)(2,1)S(1)} %add_chips.1), channel_id=1, replica_groups=mesh['fsdp'=4,'ctx'=8] {'fsdp'}, dimensions={0} | all-to-all | bytes 557056 | tf_op jit(solution)/shard_map/all_to_all | solution.py:433
  104.6 0.6 add_blocks.1
  105.2 9.3 %all-gather = bf16[2048,128]{1,0:T(8,128)(2,1)S(1)} all-gather(bf16[256,128]{1,0:T(8,128)(2,1)S(1)} %get-tuple-element.38), channel_id=2, replica_groups=mesh['fsdp'=4,'ctx'=8] {'ctx'}, dimensions={0}, use_global_device_ids=true | all-gather | bytes 589824 | tf_op jit(solution)/shard_map/all_gather | solution.py:495
  114.4 1.0 finish.1
  (5 shorter events, 0.1 us)
Async XLA Ops:
  4.7 29.7 %copy-start.3 = (f32[32]{0:T(128)S(1)}, f32[32]{0:T(128)}, u32[]{:S(2)}) copy-start(f32[32]{0:T(128)} %param.12) | copy-start | bytes 388
  4.7 29.9 %copy-start.4 = (f32[32]{0:T(128)S(1)}, f32[32]{0:T(128)}, u32[]{:S(2)}) copy-start(f32[32]{0:T(128)} %param.13) | copy-start | bytes 388
  4.7 29.9 %copy-start = (bf16[1,128,8192]{2,1,0:T(8,128)(2,1)S(1)}, bf16[1,128,8192]{2,1,0:T(8,128)(2,1)}, u32[]{:S(2)}) copy-start(bf16[1,128,8192]{2,1,0:T(8,128)(2,1)} %hidden_ref.7) | copy-start | bytes 6291460
  4.7 33.7 %all-to-all-start = ((bf16[8,1040,128]{2,1,0:T(8,128)(2,1)}), bf16[8,1040,128]{2,1,0:T(8,128)(2,1)}, u32[]{:S(2)}, u32[]{:S(2)}) async-start(bf16[8,1040,128]{2,1,0:T(8,128)(2,1)} %get-tuple-element.28), calls=%async_computation | async-start | bytes 4259840 | tf_op jit(solution)/shard_map/all_to_all | solution.py:433
  10.0 25.7 %copy-start.1 = (bf16[2048,128]{1,0:T(8,128)(2,1)S(1)}, bf16[2048,128]{1,0:T(8,128)(2,1)}, u32[]{:S(2)}) copy-start(bf16[2048,128]{1,0:T(8,128)(2,1)} %refs_0_.1) | copy-start | bytes 1572868
  10.0 14.3 %collective-permute-start = (bf16[1024,128]{1,0:T(8,128)(2,1)}, bf16[1024,128]{1,0:T(8,128)(2,1)S(1)}, u32[]{:S(2)}, u32[]{:S(2)}) collective-permute-start(bf16[1024,128]{1,0:T(8,128)(2,1)} %get-tuple-element.23), channel_id=1, source_target_pairs={{0,8},{8,0},{16,24},{24,16},{1,9},{9,1},{17,25},{25,17},{2,10},{10... | collective-permute-start | bytes 786440 | tf_op jit(solution)/shard_map/ppermute | solution.py:437
  12.3 21.6 %collective-permute-start.2 = (bf16[1024,128]{1,0:T(8,128)(2,1)}, bf16[1024,128]{1,0:T(8,128)(2,1)S(1)}, u32[]{:S(2)}, u32[]{:S(2)}) collective-permute-start(bf16[1024,128]{1,0:T(8,128)(2,1)} %get-tuple-element.23), channel_id=1, source_target_pairs={{0,16},{8,24},{16,0},{24,8},{1,17},{9,25},{17,1},{25,9},{2,18},{10... | collective-permute-start | bytes 786440 | tf_op jit(solution)/shard_map/ppermute | solution.py:437
  14.9 19.0 %collective-permute-start.4 = (bf16[1024,128]{1,0:T(8,128)(2,1)}, bf16[1024,128]{1,0:T(8,128)(2,1)S(1)}, u32[]{:S(2)}, u32[]{:S(2)}) collective-permute-start(bf16[1024,128]{1,0:T(8,128)(2,1)} %get-tuple-element.23), channel_id=1, source_target_pairs={{0,24},{8,16},{16,8},{24,0},{1,25},{9,17},{17,9},{25,1},{2,26},{10... | collective-permute-start | bytes 786440 | tf_op jit(solution)/shard_map/ppermute | solution.py:437
  24.4 12.3 %collective-permute-start.1 = (bf16[1024,128]{1,0:T(8,128)(2,1)S(1)}, bf16[1024,128]{1,0:T(8,128)(2,1)}, u32[]{:S(2)}, u32[]{:S(2)}) collective-permute-start(bf16[1024,128]{1,0:T(8,128)(2,1)S(1)} %collective-permute-done.refs_0_), channel_id=1, source_target_pairs={{0,1},{1,0},{2,3},{3,2},{4,5},{5,4},{6,7},{7,6},{8,9},{9,8},{10,11... | collective-permute-start | bytes 786440 | tf_op jit(solution)/shard_map/ppermute | solution.py:437
  33.9 2.8 %collective-permute-start.3 = (bf16[1024,128]{1,0:T(8,128)(2,1)S(1)}, bf16[1024,128]{1,0:T(8,128)(2,1)}, u32[]{:S(2)}, u32[]{:S(2)}) collective-permute-start(bf16[1024,128]{1,0:T(8,128)(2,1)S(1)} %collective-permute-done.2.refs_2_), channel_id=1, source_target_pairs={{0,1},{1,0},{2,3},{3,2},{4,5},{5,4},{6,7},{7,6},{8,9},{9,8},{10,11... | collective-permute-start | bytes 786440 | tf_op jit(solution)/shard_map/ppermute | solution.py:437
  33.9 2.8 %collective-permute-start.5 = (bf16[1024,128]{1,0:T(8,128)(2,1)S(1)}, bf16[1024,128]{1,0:T(8,128)(2,1)}, u32[]{:S(2)}, u32[]{:S(2)}) collective-permute-start(bf16[1024,128]{1,0:T(8,128)(2,1)S(1)} %collective-permute-done.4.refs_4_), channel_id=1, source_target_pairs={{0,1},{1,0},{2,3},{3,2},{4,5},{5,4},{6,7},{7,6},{8,9},{9,8},{10,11... | collective-permute-start | bytes 786440 | tf_op jit(solution)/shard_map/ppermute | solution.py:437
  34.7 1.0 copy-start.2
  48.0 22.3 %collective-permute-start.7 = (bf16[128,4096]{1,0:T(8,128)(2,1)}, bf16[128,4096]{1,0:T(8,128)(2,1)S(1)}, u32[]{:S(2)}, u32[]{:S(2)}) collective-permute-start(bf16[128,4096]{1,0:T(8,128)(2,1)} %copy-done.2), channel_id=1, source_target_pairs={{0,1},{1,0},{2,3},{3,2},{4,5},{5,4},{6,7},{7,6},{8,9},{9,8},{10,11... | collective-permute-start | bytes 3145736 | tf_op jit(solution)/shard_map/ppermute | solution.py:437
  69.0 1.3 %collective-permute-start.6 = (bf16[272,128]{1,0:T(8,128)(2,1)S(1)}, bf16[272,128]{1,0:T(8,128)(2,1)S(1)}, u32[]{:S(2)}, u32[]{:S(2)}) collective-permute-start(bf16[272,128]{1,0:T(8,128)(2,1)S(1)} %pad_maximum_fusion.near_ref), channel_id=1, source_target_pairs={{0,1},{1,0},{2,3},{3,2},{4,5},{5,4},{6,7},{7,6},{8,9},{9,8},{10,11... | collective-permute-start | bytes 208904 | tf_op jit(solution)/shard_map/ppermute | solution.py:437

commit v3 on v2

--- a/solution.py
+++ b/solution.py
@@ -465,8 +465,10 @@
     send = pack_hidden(1 - core, hidden, half)
     start = jnp.zeros((rows, both), jnp.float32)
     start = project([2 * shard, 2 * shard + 1], hidden, [proj_weight], start, jnp.float32)
+    near[0], send, rates, s_mine, start = lax.optimization_barrier(
+        (near[0], send, rates, s_mine, start)
+    )
     far = [swap(block, "ctx", 1) for block in near]
-    far, send, rates, s_mine, start = lax.optimization_barrier((far, send, rates, s_mine, start))
 
     near_at = [2 * other + core for other in others]
     far_at = [2 * other + 1 - core for other in others]

time: 116 us -> 115 us (level)
  transfers between devices with their start and end apart: 9 -> 9, of which waited for: 3 -> 5; matrix products, arithmetic and copies ran while one was open for 0% -> 0% of each run, Pallas kernels for 12% -> 12%
where the time goes in v3:
time: 115 us
  blocking collectives  61.2 us (53%)
  Pallas kernels  20.6 us (18%)
  waiting for transfers between devices  19.4 us (17%)
  starting transfers between devices  11.1 us (10%)
  local copies, waits for them, and re-layouts  1.33 us (1%)
    all_to_all x2, blocking collectives, exchange(): return lax.all_to_all(blocks, axis, 0, 0, tiled=True)  24.7 us
    ppermute x8, waiting for transfers between devices, swap(): lax.ppermute(block, axis, [(i, i ^ shift) for i in range(lax.axis_size(ax...  19.4 us
    all_to_all x1, blocking collectives, local(): lax.all_to_all(grad, 'ctx', 0, 0, tiled=True, axis_index_groups=chips)  17.6 us
    pallas_call x1, Pallas kernels, mixer(): pl.pallas_call(functools.partial(mixer_kernel, heads, scale, count), out_...  10.9 us
    all_gather x1, blocking collectives, local(): maps = lax.all_gather(projection, 'ctx', axis=0, tiled=True)  9.62 us
    all_gather x1, blocking collectives, local(): lax.all_gather(grad, 'ctx', axis=0)  9.28 us
    ppermute x8, starting transfers between devices, swap(): lax.ppermute(block, axis, [(i, i ^ shift) for i in range(lax.axis_size(ax...  5.81 us
    all_to_all x1, starting transfers between devices, exchange(): return lax.all_to_all(blocks, axis, 0, 0, tiled=True)  5.31 us
  transfers between devices with their start and end apart: 9, of which 5 were waited for; matrix products, arithmetic and copies ran while one was open for 0% of the time, Pallas kernels for 12%

profile of v3, /device:TPU:0, one launch (start us, length us, event | category | flops | bytes accessed | tf_op | source)
XLA Modules:
  0.0 114.7 jit_solution(7783007267447539160)
XLA Ops:
  0.6 4.1 %pack_mixer.1 = (bf16[8,1040,128]{2,1,0:T(8,128)(2,1)}, bf16[1024,128]{1,0:T(8,128)(2,1)}) custom-call(s32[1]{0:T(128)} %bitcast.core_ref, bf16[1,128,4096]{2,1,0:T(8,128)(2,1)} %values_hbm.1, bf16[1,128,4096]{2,1,0:T(8,128)(2,1)} %targets_hbm.1, f32[1,32,128]{2,1,0:T(8,128)} %dt_ref.1, bf16[2048,128]{1,0:T(8,128)(2,1)} %refs_0_.1), custom_call_target="tpu_custom_call" | custom-call | tf_op jit(solution)/shard_map/pack_mixer/pallas_call | solution.py:261
  4.7 0.0 copy-start.3
  4.7 0.0 copy-start.4
  4.7 0.0 copy-start
  4.7 5.3 %all-to-all-start = ((bf16[8,1040,128]{2,1,0:T(8,128)(2,1)}), bf16[8,1040,128]{2,1,0:T(8,128)(2,1)}, u32[]{:S(2)}, u32[]{:S(2)}) async-start(bf16[8,1040,128]{2,1,0:T(8,128)(2,1)} %get-tuple-element.24), calls=%async_computation | async-start | bytes 4259840 | tf_op jit(solution)/shard_map/all_to_all | solution.py:433
  10.1 0.0 copy-start.1
  10.1 2.3 %collective-permute-start = (bf16[1024,128]{1,0:T(8,128)(2,1)}, bf16[1024,128]{1,0:T(8,128)(2,1)S(1)}, u32[]{:S(2)}, u32[]{:S(2)}) collective-permute-start(bf16[1024,128]{1,0:T(8,128)(2,1)} %get-tuple-element.21), channel_id=1, source_target_pairs={{0,8},{8,0},{16,24},{24,16},{1,9},{9,1},{17,25},{25,17},{2,10},{10... | collective-permute-start | bytes 786440 | tf_op jit(solution)/shard_map/ppermute | solution.py:437
  12.3 2.6 %collective-permute-start.2 = (bf16[1024,128]{1,0:T(8,128)(2,1)}, bf16[1024,128]{1,0:T(8,128)(2,1)S(1)}, u32[]{:S(2)}, u32[]{:S(2)}) collective-permute-start(bf16[1024,128]{1,0:T(8,128)(2,1)} %get-tuple-element.21), channel_id=1, source_target_pairs={{0,16},{8,24},{16,0},{24,8},{1,17},{9,25},{17,1},{25,9},{2,18},{10... | collective-permute-start | bytes 786440 | tf_op jit(solution)/shard_map/ppermute | solution.py:437
  14.9 0.0 collective-permute-start.4
  14.9 0.0 copy-done.3
  14.9 0.1 exponential_negate_fusion
  15.0 0.1 broadcast_in_dim_tile.3
  15.1 0.0 copy-done.4
  15.1 0.1 dynamic_slice.7.skip_ref
  15.2 0.0 copy-done
  15.2 0.1 pack_hidden.1
  15.3 0.0 copy-start.2
  15.3 1.0 copy-done.2
  16.2 0.1 pad_add_fusion.chunk_ref
  16.3 0.0 copy-done.1
  16.3 0.8 project.2.start_ref
  17.2 7.3 %collective-permute-done.refs_0_ = bf16[1024,128]{1,0:T(8,128)(2,1)S(1)} collective-permute-done((bf16[1024,128]{1,0:T(8,128)(2,1)}, bf16[1024,128]{1,0:T(8,128)(2,1)S(1)}, u32[]{:S(2)}, u32[]{:S(2)}) %collective-permute-start) | collective-permute-done | bytes 262176 | tf_op jit(solution)/shard_map/ppermute | solution.py:437
  24.4 0.0 collective-permute-start.1
  24.4 9.5 %collective-permute-done.2.refs_2_ = bf16[1024,128]{1,0:T(8,128)(2,1)S(1)} collective-permute-done((bf16[1024,128]{1,0:T(8,128)(2,1)}, bf16[1024,128]{1,0:T(8,128)(2,1)S(1)}, u32[]{:S(2)}, u32[]{:S(2)}) %collective-permute-start.2) | collective-permute-done | bytes 262176 | tf_op jit(solution)/shard_map/ppermute | solution.py:437
  33.9 0.0 collective-permute-start.3
  33.9 0.0 collective-permute-done.4.refs_4_
  33.9 0.5 collective-permute-start.5
  34.4 0.1 stack.36.chunk_ref
  34.5 0.0 collective-permute-done.1.refs_1_
  34.5 1.2 %collective-permute-done.3.refs_3_ = bf16[1024,128]{1,0:T(8,128)(2,1)S(1)} collective-permute-done((bf16[1024,128]{1,0:T(8,128)(2,1)S(1)}, bf16[1024,128]{1,0:T(8,128)(2,1)S(1)}, u32[]{:S(2)}, u32[]{:S(2)}) %collective-permute-start.3) | collective-permute-done | bytes 262176 | tf_op jit(solution)/shard_map/ppermute | solution.py:437
  35.7 0.2 collective-permute-done.5.refs_5_
  35.9 1.5 %project.3 = bf16[128,128]{1,0:T(8,128)(2,1)S(1)} custom-call(s32[6]{0:T(128)S(1)} %stack.36.chunk_ref, bf16[1,128,8192]{2,1,0:T(8,128)(2,1)S(1)} %copy-done, f32[128,128]{1,0:T(8,128)S(1)} %project.2.start_ref, bf16[1024,128]{1,0:T(8,128)(2,1)S(1)} %collective-permute-done.refs_0_, bf16[1024,128]{1,0:T(8,128)(2,1)S(1)} %collective-permute-done.1.refs_1_, ...), custom_call_target="tpu_custom_call" | custom-call | tf_op jit(solution)/shard_map/project/pallas_call | solution.py:313
  37.5 0.0 all-to-all-done.vt_hbm
  37.5 9.6 %all_gather.9.maps_ref = bf16[1024,128]{1,0:T(8,128)(2,1)S(1)} all-gather(bf16[128,128]{1,0:T(8,128)(2,1)S(1)} %project.3), channel_id=1, replica_groups=mesh['fsdp'=4,'ctx'=8] {'ctx'}, dimensions={0}, use_global_device_ids=true | all-gather | bytes 294912 | tf_op jit(solution)/shard_map/all_gather | solution.py:479
  47.1 0.4 collective-permute-start.7
  47.5 0.1 copy.12.rate_ref
  47.5 10.9 %mixer.1 = (bf16[1024,128]{1,0:T(8,128)(2,1)S(1)}, bf16[16,128]{1,0:T(8,128)(2,1)S(1)}) custom-call(bf16[1024,128]{1,0:T(8,128)(2,1)S(1)} %all_gather.9.maps_ref, bf16[8,1040,128]{2,1,0:T(8,128)(2,1)} %all-to-all-done.vt_hbm, f32[32,1]{1,0:T(8,128)S(1)} %copy.12.rate_ref, f32[4]{0:T(128)S(1)} %dynamic_slice.7.skip_ref, s32[1]{0:T(128)} %bitcast.10.first_ref), custom_call_target="tpu_custom_call" | custom-call | flops 939524096 | bytes 3145728 | tf_op jit(solution)/shard_map/mixer/pallas_call | solution.py:194
  58.5 9.5 %all_to_all.20 = bf16[8,128,128]{2,1,0:T(8,128)(2,1)S(1)} all-to-all(bf16[8,128,128]{2,1,0:T(8,128)(2,1)S(1)} %bitcast.18), channel_id=1, replica_groups=mesh['fsdp'=4,'ctx'=8] {'ctx'}, dimensions={0} | all-to-all | bytes 524288 | tf_op jit(solution)/shard_map/all_to_all | solution.py:433
  68.1 0.1 collective-permute-start.6
  68.1 1.2 %collective-permute-done.6.far_ref = bf16[272,128]{1,0:T(8,128)(2,1)S(1)} collective-permute-done((bf16[272,128]{1,0:T(8,128)(2,1)S(1)}, bf16[272,128]{1,0:T(8,128)(2,1)S(1)}, u32[]{:S(2)}, u32[]{:S(2)}) %collective-permute-start.6) | collective-permute-done | bytes 69664 | tf_op jit(solution)/shard_map/ppermute | solution.py:437
  69.4 0.0 collective-permute-done.7.feats_ref
  69.4 1.3 %weight_grad.1 = bf16[4,1040,128]{2,1,0:T(8,128)(2,1)S(1)} custom-call(s32[1]{0:T(128)} %bitcast.core_ref, bf16[272,128]{1,0:T(8,128)(2,1)S(1)} %pad_maximum_fusion.near_ref, bf16[272,128]{1,0:T(8,128)(2,1)S(1)} %collective-permute-done.6.far_ref, bf16[1,128,8192]{2,1,0:T(8,128)(2,1)S(1)} %copy-done, bf16[128,4096]{1,0:T(8,128)(2,1)S(1)} %collective-permute-done.7.feats_ref), custom_call_target="tpu_custom_call" | custom-call | tf_op jit(solution)/shard_map/weight_grad/pallas_call | solution.py:356
  70.7 17.6 %all_to_all.21.grad_ref = bf16[4,1040,128]{2,1,0:T(8,128)(2,1)S(1)} all-to-all(bf16[4,1040,128]{2,1,0:T(8,128)(2,1)S(1)} %weight_grad.1), channel_id=1, replica_groups={{0,2,4,6},{1,3,5,7},{8,10,12,14},{9,11,13,15},{16,18,20,22},{17,19,21,2..., dimensions={0} | all-to-all | bytes 2129920 | tf_op jit(solution)/shard_map/all_to_all | solution.py:494
  88.4 0.2 add_chips.1
  88.6 15.2 %all_to_all.22.grad_ref = bf16[4,272,128]{2,1,0:T(8,128)(2,1)S(1)} all-to-all(bf16[4,272,128]{2,1,0:T(8,128)(2,1)S(1)} %add_chips.1), channel_id=1, replica_groups=mesh['fsdp'=4,'ctx'=8] {'fsdp'}, dimensions={0} | all-to-all | bytes 557056 | tf_op jit(solution)/shard_map/all_to_all | solution.py:433
  103.8 0.6 add_blocks.1
  104.3 9.3 %all-gather = bf16[2048,128]{1,0:T(8,128)(2,1)S(1)} all-gather(bf16[256,128]{1,0:T(8,128)(2,1)S(1)} %get-tuple-element.34), channel_id=2, replica_groups=mesh['fsdp'=4,'ctx'=8] {'ctx'}, dimensions={0}, use_global_device_ids=true | all-gather | bytes 589824 | tf_op jit(solution)/shard_map/all_gather | solution.py:497
  113.6 1.0 finish.1
  (5 shorter events, 0.1 us)
Async XLA Ops:
  4.7 10.2 %copy-start.3 = (f32[32]{0:T(128)S(1)}, f32[32]{0:T(128)}, u32[]{:S(2)}) copy-start(f32[32]{0:T(128)} %param.12) | copy-start | bytes 388
  4.7 10.4 %copy-start.4 = (f32[32]{0:T(128)S(1)}, f32[32]{0:T(128)}, u32[]{:S(2)}) copy-start(f32[32]{0:T(128)} %param.13) | copy-start | bytes 388
  4.7 10.4 %copy-start = (bf16[1,128,8192]{2,1,0:T(8,128)(2,1)S(1)}, bf16[1,128,8192]{2,1,0:T(8,128)(2,1)}, u32[]{:S(2)}) copy-start(bf16[1,128,8192]{2,1,0:T(8,128)(2,1)} %hidden_ref.7) | copy-start | bytes 6291460
  4.7 32.7 %all-to-all-start = ((bf16[8,1040,128]{2,1,0:T(8,128)(2,1)}), bf16[8,1040,128]{2,1,0:T(8,128)(2,1)}, u32[]{:S(2)}, u32[]{:S(2)}) async-start(bf16[8,1040,128]{2,1,0:T(8,128)(2,1)} %get-tuple-element.24), calls=%async_computation | async-start | bytes 4259840 | tf_op jit(solution)/shard_map/all_to_all | solution.py:433
  10.1 6.3 %copy-start.1 = (bf16[2048,128]{1,0:T(8,128)(2,1)S(1)}, bf16[2048,128]{1,0:T(8,128)(2,1)}, u32[]{:S(2)}) copy-start(bf16[2048,128]{1,0:T(8,128)(2,1)} %refs_0_.1) | copy-start | bytes 1572868
  10.1 14.3 %collective-permute-start = (bf16[1024,128]{1,0:T(8,128)(2,1)}, bf16[1024,128]{1,0:T(8,128)(2,1)S(1)}, u32[]{:S(2)}, u32[]{:S(2)}) collective-permute-start(bf16[1024,128]{1,0:T(8,128)(2,1)} %get-tuple-element.21), channel_id=1, source_target_pairs={{0,8},{8,0},{16,24},{24,16},{1,9},{9,1},{17,25},{25,17},{2,10},{10... | collective-permute-start | bytes 786440 | tf_op jit(solution)/shard_map/ppermute | solution.py:437
  12.3 21.6 %collective-permute-start.2 = (bf16[1024,128]{1,0:T(8,128)(2,1)}, bf16[1024,128]{1,0:T(8,128)(2,1)S(1)}, u32[]{:S(2)}, u32[]{:S(2)}) collective-permute-start(bf16[1024,128]{1,0:T(8,128)(2,1)} %get-tuple-element.21), channel_id=1, source_target_pairs={{0,16},{8,24},{16,0},{24,8},{1,17},{9,25},{17,1},{25,9},{2,18},{10... | collective-permute-start | bytes 786440 | tf_op jit(solution)/shard_map/ppermute | solution.py:437
  14.9 19.0 %collective-permute-start.4 = (bf16[1024,128]{1,0:T(8,128)(2,1)}, bf16[1024,128]{1,0:T(8,128)(2,1)S(1)}, u32[]{:S(2)}, u32[]{:S(2)}) collective-permute-start(bf16[1024,128]{1,0:T(8,128)(2,1)} %get-tuple-element.21), channel_id=1, source_target_pairs={{0,24},{8,16},{16,8},{24,0},{1,25},{9,17},{17,9},{25,1},{2,26},{10... | collective-permute-start | bytes 786440 | tf_op jit(solution)/shard_map/ppermute | solution.py:437
  15.3 1.0 copy-start.2
  24.4 10.1 %collective-permute-start.1 = (bf16[1024,128]{1,0:T(8,128)(2,1)S(1)}, bf16[1024,128]{1,0:T(8,128)(2,1)S(1)}, u32[]{:S(2)}, u32[]{:S(2)}) collective-permute-start(bf16[1024,128]{1,0:T(8,128)(2,1)S(1)} %collective-permute-done.refs_0_), channel_id=1, source_target_pairs={{0,1},{1,0},{2,3},{3,2},{4,5},{5,4},{6,7},{7,6},{8,9},{9,8},{10,11... | collective-permute-start | bytes 786440 | tf_op jit(solution)/shard_map/ppermute | solution.py:437
  33.9 1.8 %collective-permute-start.3 = (bf16[1024,128]{1,0:T(8,128)(2,1)S(1)}, bf16[1024,128]{1,0:T(8,128)(2,1)S(1)}, u32[]{:S(2)}, u32[]{:S(2)}) collective-permute-start(bf16[1024,128]{1,0:T(8,128)(2,1)S(1)} %collective-permute-done.2.refs_2_), channel_id=1, source_target_pairs={{0,1},{1,0},{2,3},{3,2},{4,5},{5,4},{6,7},{7,6},{8,9},{9,8},{10,11... | collective-permute-start | bytes 786440 | tf_op jit(solution)/shard_map/ppermute | solution.py:437
  33.9 2.0 %collective-permute-start.5 = (bf16[1024,128]{1,0:T(8,128)(2,1)S(1)}, bf16[1024,128]{1,0:T(8,128)(2,1)}, u32[]{:S(2)}, u32[]{:S(2)}) collective-permute-start(bf16[1024,128]{1,0:T(8,128)(2,1)S(1)} %collective-permute-done.4.refs_4_), channel_id=1, source_target_pairs={{0,1},{1,0},{2,3},{3,2},{4,5},{5,4},{6,7},{7,6},{8,9},{9,8},{10,11... | collective-permute-start | bytes 786440 | tf_op jit(solution)/shard_map/ppermute | solution.py:437
  47.1 22.3 %collective-permute-start.7 = (bf16[128,4096]{1,0:T(8,128)(2,1)}, bf16[128,4096]{1,0:T(8,128)(2,1)S(1)}, u32[]{:S(2)}, u32[]{:S(2)}) collective-permute-start(bf16[128,4096]{1,0:T(8,128)(2,1)} %copy-done.2), channel_id=1, source_target_pairs={{0,1},{1,0},{2,3},{3,2},{4,5},{5,4},{6,7},{7,6},{8,9},{9,8},{10,11... | collective-permute-start | bytes 3145736 | tf_op jit(solution)/shard_map/ppermute | solution.py:437
  68.1 1.3 %collective-permute-start.6 = (bf16[272,128]{1,0:T(8,128)(2,1)S(1)}, bf16[272,128]{1,0:T(8,128)(2,1)S(1)}, u32[]{:S(2)}, u32[]{:S(2)}) collective-permute-start(bf16[272,128]{1,0:T(8,128)(2,1)S(1)} %pad_maximum_fusion.near_ref), channel_id=1, source_target_pairs={{0,1},{1,0},{2,3},{3,2},{4,5},{5,4},{6,7},{7,6},{8,9},{9,8},{10,11... | collective-permute-start | bytes 208904 | tf_op jit(solution)/shard_map/ppermute | solution.py:437

commit v4 on v3

--- a/solution.py
+++ b/solution.py
@@ -170,7 +170,7 @@
 
 
 def unrolled(count, step, start):
-    each = 4 if count % 4 == 0 else 1
+    each = 2 if count % 2 == 0 else 1
 
     def several(i, value):
         for j in range(each):

time: 115 us -> 115 us (level)
  no operation moved by 1% of the time
where the time goes in v4:
time: 115 us
  blocking collectives  61.2 us (53%)
  Pallas kernels  20.9 us (18%)
  waiting for transfers between devices  19.4 us (17%)
  starting transfers between devices  11.1 us (10%)
  local copies, waits for them, and re-layouts  1.33 us (1%)
    all_to_all x2, blocking collectives, exchange(): return lax.all_to_all(blocks, axis, 0, 0, tiled=True)  24.7 us
    ppermute x8, waiting for transfers between devices, swap(): lax.ppermute(block, axis, [(i, i ^ shift) for i in range(lax.axis_size(ax...  19.4 us
    all_to_all x1, blocking collectives, local(): lax.all_to_all(grad, 'ctx', 0, 0, tiled=True, axis_index_groups=chips)  17.6 us
    pallas_call x1, Pallas kernels, mixer(): pl.pallas_call(functools.partial(mixer_kernel, heads, scale, count), out_...  11.2 us
    all_gather x1, blocking collectives, local(): maps = lax.all_gather(projection, 'ctx', axis=0, tiled=True)  9.62 us
    all_gather x1, blocking collectives, local(): lax.all_gather(grad, 'ctx', axis=0)  9.28 us
    ppermute x8, starting transfers between devices, swap(): lax.ppermute(block, axis, [(i, i ^ shift) for i in range(lax.axis_size(ax...  5.81 us
    all_to_all x1, starting transfers between devices, exchange(): return lax.all_to_all(blocks, axis, 0, 0, tiled=True)  5.31 us
  transfers between devices with their start and end apart: 9, of which 5 were waited for; matrix products, arithmetic and copies ran while one was open for 0% of the time, Pallas kernels for 12%

profile of v4, /device:TPU:0, one launch (start us, length us, event | category | flops | bytes accessed | tf_op | source)
XLA Modules:
  0.0 114.9 jit_solution(10349127657377672046)
XLA Ops:
  0.6 4.1 %pack_mixer.1 = (bf16[8,1040,128]{2,1,0:T(8,128)(2,1)}, bf16[1024,128]{1,0:T(8,128)(2,1)}) custom-call(s32[1]{0:T(128)} %bitcast.core_ref, bf16[1,128,4096]{2,1,0:T(8,128)(2,1)} %values_hbm.1, bf16[1,128,4096]{2,1,0:T(8,128)(2,1)} %targets_hbm.1, f32[1,32,128]{2,1,0:T(8,128)} %dt_ref.1, bf16[2048,128]{1,0:T(8,128)(2,1)} %refs_0_.1), custom_call_target="tpu_custom_call" | custom-call | tf_op jit(solution)/shard_map/pack_mixer/pallas_call | solution.py:261
  4.7 0.0 copy-start.3
  4.7 0.0 copy-start.4
  4.7 0.0 copy-start
  4.7 5.3 %all-to-all-start = ((bf16[8,1040,128]{2,1,0:T(8,128)(2,1)}), bf16[8,1040,128]{2,1,0:T(8,128)(2,1)}, u32[]{:S(2)}, u32[]{:S(2)}) async-start(bf16[8,1040,128]{2,1,0:T(8,128)(2,1)} %get-tuple-element.24), calls=%async_computation | async-start | bytes 4259840 | tf_op jit(solution)/shard_map/all_to_all | solution.py:433
  10.1 0.0 copy-start.1
  10.1 2.3 %collective-permute-start = (bf16[1024,128]{1,0:T(8,128)(2,1)}, bf16[1024,128]{1,0:T(8,128)(2,1)S(1)}, u32[]{:S(2)}, u32[]{:S(2)}) collective-permute-start(bf16[1024,128]{1,0:T(8,128)(2,1)} %get-tuple-element.21), channel_id=1, source_target_pairs={{0,8},{8,0},{16,24},{24,16},{1,9},{9,1},{17,25},{25,17},{2,10},{10... | collective-permute-start | bytes 786440 | tf_op jit(solution)/shard_map/ppermute | solution.py:437
  12.3 2.6 %collective-permute-start.2 = (bf16[1024,128]{1,0:T(8,128)(2,1)}, bf16[1024,128]{1,0:T(8,128)(2,1)S(1)}, u32[]{:S(2)}, u32[]{:S(2)}) collective-permute-start(bf16[1024,128]{1,0:T(8,128)(2,1)} %get-tuple-element.21), channel_id=1, source_target_pairs={{0,16},{8,24},{16,0},{24,8},{1,17},{9,25},{17,1},{25,9},{2,18},{10... | collective-permute-start | bytes 786440 | tf_op jit(solution)/shard_map/ppermute | solution.py:437
  14.9 0.0 collective-permute-start.4
  14.9 0.0 copy-done.3
  14.9 0.1 exponential_negate_fusion
  15.0 0.1 broadcast_in_dim_tile.3
  15.1 0.0 copy-done.4
  15.1 0.1 dynamic_slice.7.skip_ref
  15.2 0.0 copy-done
  15.2 0.1 pack_hidden.1
  15.3 0.0 copy-start.2
  15.3 1.0 copy-done.2
  16.2 0.1 pad_add_fusion.chunk_ref
  16.3 0.0 copy-done.1
  16.3 0.8 project.2.start_ref
  17.2 7.3 %collective-permute-done.refs_0_ = bf16[1024,128]{1,0:T(8,128)(2,1)S(1)} collective-permute-done((bf16[1024,128]{1,0:T(8,128)(2,1)}, bf16[1024,128]{1,0:T(8,128)(2,1)S(1)}, u32[]{:S(2)}, u32[]{:S(2)}) %collective-permute-start) | collective-permute-done | bytes 262176 | tf_op jit(solution)/shard_map/ppermute | solution.py:437
  24.4 0.0 collective-permute-start.1
  24.4 9.5 %collective-permute-done.2.refs_2_ = bf16[1024,128]{1,0:T(8,128)(2,1)S(1)} collective-permute-done((bf16[1024,128]{1,0:T(8,128)(2,1)}, bf16[1024,128]{1,0:T(8,128)(2,1)S(1)}, u32[]{:S(2)}, u32[]{:S(2)}) %collective-permute-start.2) | collective-permute-done | bytes 262176 | tf_op jit(solution)/shard_map/ppermute | solution.py:437
  33.9 0.0 collective-permute-start.3
  33.9 0.0 collective-permute-done.4.refs_4_
  33.9 0.5 collective-permute-start.5
  34.4 0.1 stack.36.chunk_ref
  34.5 0.0 collective-permute-done.1.refs_1_
  34.5 1.2 %collective-permute-done.3.refs_3_ = bf16[1024,128]{1,0:T(8,128)(2,1)S(1)} collective-permute-done((bf16[1024,128]{1,0:T(8,128)(2,1)S(1)}, bf16[1024,128]{1,0:T(8,128)(2,1)S(1)}, u32[]{:S(2)}, u32[]{:S(2)}) %collective-permute-start.3) | collective-permute-done | bytes 262176 | tf_op jit(solution)/shard_map/ppermute | solution.py:437
  35.7 0.2 collective-permute-done.5.refs_5_
  35.9 1.5 %project.3 = bf16[128,128]{1,0:T(8,128)(2,1)S(1)} custom-call(s32[6]{0:T(128)S(1)} %stack.36.chunk_ref, bf16[1,128,8192]{2,1,0:T(8,128)(2,1)S(1)} %copy-done, f32[128,128]{1,0:T(8,128)S(1)} %project.2.start_ref, bf16[1024,128]{1,0:T(8,128)(2,1)S(1)} %collective-permute-done.refs_0_, bf16[1024,128]{1,0:T(8,128)(2,1)S(1)} %collective-permute-done.1.refs_1_, ...), custom_call_target="tpu_custom_call" | custom-call | tf_op jit(solution)/shard_map/project/pallas_call | solution.py:313
  37.5 0.0 all-to-all-done.vt_hbm
  37.5 9.6 %all_gather.9.maps_ref = bf16[1024,128]{1,0:T(8,128)(2,1)S(1)} all-gather(bf16[128,128]{1,0:T(8,128)(2,1)S(1)} %project.3), channel_id=1, replica_groups=mesh['fsdp'=4,'ctx'=8] {'ctx'}, dimensions={0}, use_global_device_ids=true | all-gather | bytes 294912 | tf_op jit(solution)/shard_map/all_gather | solution.py:479
  47.1 0.4 collective-permute-start.7
  47.5 0.1 copy.12.rate_ref
  47.5 11.2 %mixer.1 = (bf16[1024,128]{1,0:T(8,128)(2,1)S(1)}, bf16[16,128]{1,0:T(8,128)(2,1)S(1)}) custom-call(bf16[1024,128]{1,0:T(8,128)(2,1)S(1)} %all_gather.9.maps_ref, bf16[8,1040,128]{2,1,0:T(8,128)(2,1)} %all-to-all-done.vt_hbm, f32[32,1]{1,0:T(8,128)S(1)} %copy.12.rate_ref, f32[4]{0:T(128)S(1)} %dynamic_slice.7.skip_ref, s32[1]{0:T(128)} %bitcast.10.first_ref), custom_call_target="tpu_custom_call" | custom-call | flops 939524096 | bytes 3145728 | tf_op jit(solution)/shard_map/mixer/pallas_call | solution.py:194
  58.7 9.5 %all_to_all.20 = bf16[8,128,128]{2,1,0:T(8,128)(2,1)S(1)} all-to-all(bf16[8,128,128]{2,1,0:T(8,128)(2,1)S(1)} %bitcast.18), channel_id=1, replica_groups=mesh['fsdp'=4,'ctx'=8] {'ctx'}, dimensions={0} | all-to-all | bytes 524288 | tf_op jit(solution)/shard_map/all_to_all | solution.py:433
  68.3 0.1 collective-permute-start.6
  68.4 1.2 %collective-permute-done.6.far_ref = bf16[272,128]{1,0:T(8,128)(2,1)S(1)} collective-permute-done((bf16[272,128]{1,0:T(8,128)(2,1)S(1)}, bf16[272,128]{1,0:T(8,128)(2,1)S(1)}, u32[]{:S(2)}, u32[]{:S(2)}) %collective-permute-start.6) | collective-permute-done | bytes 69664 | tf_op jit(solution)/shard_map/ppermute | solution.py:437
  69.6 0.0 collective-permute-done.7.feats_ref
  69.6 1.3 %weight_grad.1 = bf16[4,1040,128]{2,1,0:T(8,128)(2,1)S(1)} custom-call(s32[1]{0:T(128)} %bitcast.core_ref, bf16[272,128]{1,0:T(8,128)(2,1)S(1)} %pad_maximum_fusion.near_ref, bf16[272,128]{1,0:T(8,128)(2,1)S(1)} %collective-permute-done.6.far_ref, bf16[1,128,8192]{2,1,0:T(8,128)(2,1)S(1)} %copy-done, bf16[128,4096]{1,0:T(8,128)(2,1)S(1)} %collective-permute-done.7.feats_ref), custom_call_target="tpu_custom_call" | custom-call | tf_op jit(solution)/shard_map/weight_grad/pallas_call | solution.py:356
  71.0 17.6 %all_to_all.21.grad_ref = bf16[4,1040,128]{2,1,0:T(8,128)(2,1)S(1)} all-to-all(bf16[4,1040,128]{2,1,0:T(8,128)(2,1)S(1)} %weight_grad.1), channel_id=1, replica_groups={{0,2,4,6},{1,3,5,7},{8,10,12,14},{9,11,13,15},{16,18,20,22},{17,19,21,2..., dimensions={0} | all-to-all | bytes 2129920 | tf_op jit(solution)/shard_map/all_to_all | solution.py:494
  88.6 0.2 add_chips.1
  88.8 15.2 %all_to_all.22.grad_ref = bf16[4,272,128]{2,1,0:T(8,128)(2,1)S(1)} all-to-all(bf16[4,272,128]{2,1,0:T(8,128)(2,1)S(1)} %add_chips.1), channel_id=1, replica_groups=mesh['fsdp'=4,'ctx'=8] {'fsdp'}, dimensions={0} | all-to-all | bytes 557056 | tf_op jit(solution)/shard_map/all_to_all | solution.py:433
  104.0 0.6 add_blocks.1
  104.6 9.3 %all-gather = bf16[2048,128]{1,0:T(8,128)(2,1)S(1)} all-gather(bf16[256,128]{1,0:T(8,128)(2,1)S(1)} %get-tuple-element.34), channel_id=2, replica_groups=mesh['fsdp'=4,'ctx'=8] {'ctx'}, dimensions={0}, use_global_device_ids=true | all-gather | bytes 589824 | tf_op jit(solution)/shard_map/all_gather | solution.py:497
  113.9 1.0 finish.1
  (5 shorter events, 0.1 us)
Async XLA Ops:
  4.7 10.2 %copy-start.3 = (f32[32]{0:T(128)S(1)}, f32[32]{0:T(128)}, u32[]{:S(2)}) copy-start(f32[32]{0:T(128)} %param.12) | copy-start | bytes 388
  4.7 10.4 %copy-start.4 = (f32[32]{0:T(128)S(1)}, f32[32]{0:T(128)}, u32[]{:S(2)}) copy-start(f32[32]{0:T(128)} %param.13) | copy-start | bytes 388
  4.7 10.4 %copy-start = (bf16[1,128,8192]{2,1,0:T(8,128)(2,1)S(1)}, bf16[1,128,8192]{2,1,0:T(8,128)(2,1)}, u32[]{:S(2)}) copy-start(bf16[1,128,8192]{2,1,0:T(8,128)(2,1)} %hidden_ref.7) | copy-start | bytes 6291460
  4.7 32.7 %all-to-all-start = ((bf16[8,1040,128]{2,1,0:T(8,128)(2,1)}), bf16[8,1040,128]{2,1,0:T(8,128)(2,1)}, u32[]{:S(2)}, u32[]{:S(2)}) async-start(bf16[8,1040,128]{2,1,0:T(8,128)(2,1)} %get-tuple-element.24), calls=%async_computation | async-start | bytes 4259840 | tf_op jit(solution)/shard_map/all_to_all | solution.py:433
  10.1 6.3 %copy-start.1 = (bf16[2048,128]{1,0:T(8,128)(2,1)S(1)}, bf16[2048,128]{1,0:T(8,128)(2,1)}, u32[]{:S(2)}) copy-start(bf16[2048,128]{1,0:T(8,128)(2,1)} %refs_0_.1) | copy-start | bytes 1572868
  10.1 14.3 %collective-permute-start = (bf16[1024,128]{1,0:T(8,128)(2,1)}, bf16[1024,128]{1,0:T(8,128)(2,1)S(1)}, u32[]{:S(2)}, u32[]{:S(2)}) collective-permute-start(bf16[1024,128]{1,0:T(8,128)(2,1)} %get-tuple-element.21), channel_id=1, source_target_pairs={{0,8},{8,0},{16,24},{24,16},{1,9},{9,1},{17,25},{25,17},{2,10},{10... | collective-permute-start | bytes 786440 | tf_op jit(solution)/shard_map/ppermute | solution.py:437
  12.3 21.6 %collective-permute-start.2 = (bf16[1024,128]{1,0:T(8,128)(2,1)}, bf16[1024,128]{1,0:T(8,128)(2,1)S(1)}, u32[]{:S(2)}, u32[]{:S(2)}) collective-permute-start(bf16[1024,128]{1,0:T(8,128)(2,1)} %get-tuple-element.21), channel_id=1, source_target_pairs={{0,16},{8,24},{16,0},{24,8},{1,17},{9,25},{17,1},{25,9},{2,18},{10... | collective-permute-start | bytes 786440 | tf_op jit(solution)/shard_map/ppermute | solution.py:437
  14.9 19.0 %collective-permute-start.4 = (bf16[1024,128]{1,0:T(8,128)(2,1)}, bf16[1024,128]{1,0:T(8,128)(2,1)S(1)}, u32[]{:S(2)}, u32[]{:S(2)}) collective-permute-start(bf16[1024,128]{1,0:T(8,128)(2,1)} %get-tuple-element.21), channel_id=1, source_target_pairs={{0,24},{8,16},{16,8},{24,0},{1,25},{9,17},{17,9},{25,1},{2,26},{10... | collective-permute-start | bytes 786440 | tf_op jit(solution)/shard_map/ppermute | solution.py:437
  15.3 1.0 copy-start.2
  24.4 10.1 %collective-permute-start.1 = (bf16[1024,128]{1,0:T(8,128)(2,1)S(1)}, bf16[1024,128]{1,0:T(8,128)(2,1)S(1)}, u32[]{:S(2)}, u32[]{:S(2)}) collective-permute-start(bf16[1024,128]{1,0:T(8,128)(2,1)S(1)} %collective-permute-done.refs_0_), channel_id=1, source_target_pairs={{0,1},{1,0},{2,3},{3,2},{4,5},{5,4},{6,7},{7,6},{8,9},{9,8},{10,11... | collective-permute-start | bytes 786440 | tf_op jit(solution)/shard_map/ppermute | solution.py:437
  33.9 1.8 %collective-permute-start.3 = (bf16[1024,128]{1,0:T(8,128)(2,1)S(1)}, bf16[1024,128]{1,0:T(8,128)(2,1)S(1)}, u32[]{:S(2)}, u32[]{:S(2)}) collective-permute-start(bf16[1024,128]{1,0:T(8,128)(2,1)S(1)} %collective-permute-done.2.refs_2_), channel_id=1, source_target_pairs={{0,1},{1,0},{2,3},{3,2},{4,5},{5,4},{6,7},{7,6},{8,9},{9,8},{10,11... | collective-permute-start | bytes 786440 | tf_op jit(solution)/shard_map/ppermute | solution.py:437
  33.9 2.0 %collective-permute-start.5 = (bf16[1024,128]{1,0:T(8,128)(2,1)S(1)}, bf16[1024,128]{1,0:T(8,128)(2,1)}, u32[]{:S(2)}, u32[]{:S(2)}) collective-permute-start(bf16[1024,128]{1,0:T(8,128)(2,1)S(1)} %collective-permute-done.4.refs_4_), channel_id=1, source_target_pairs={{0,1},{1,0},{2,3},{3,2},{4,5},{5,4},{6,7},{7,6},{8,9},{9,8},{10,11... | collective-permute-start | bytes 786440 | tf_op jit(solution)/shard_map/ppermute | solution.py:437
  47.1 22.5 %collective-permute-start.7 = (bf16[128,4096]{1,0:T(8,128)(2,1)}, bf16[128,4096]{1,0:T(8,128)(2,1)S(1)}, u32[]{:S(2)}, u32[]{:S(2)}) collective-permute-start(bf16[128,4096]{1,0:T(8,128)(2,1)} %copy-done.2), channel_id=1, source_target_pairs={{0,1},{1,0},{2,3},{3,2},{4,5},{5,4},{6,7},{7,6},{8,9},{9,8},{10,11... | collective-permute-start | bytes 3145736 | tf_op jit(solution)/shard_map/ppermute | solution.py:437
  68.3 1.3 %collective-permute-start.6 = (bf16[272,128]{1,0:T(8,128)(2,1)S(1)}, bf16[272,128]{1,0:T(8,128)(2,1)S(1)}, u32[]{:S(2)}, u32[]{:S(2)}) collective-permute-start(bf16[272,128]{1,0:T(8,128)(2,1)S(1)} %pad_maximum_fusion.near_ref), channel_id=1, source_target_pairs={{0,1},{1,0},{2,3},{3,2},{4,5},{5,4},{6,7},{7,6},{8,9},{9,8},{10,11... | collective-permute-start | bytes 208904 | tf_op jit(solution)/shard_map/ppermute | solution.py:437
